TPU v7x, 512 devices: a whole 4x8x8 slice. The times are simulated.
512 devices in a mesh: wide: 64 (over z, y), narrow: 8 (over x, core).
Axes of the slice: x: 4, y: 8, z: 8, core: 2. Of those that a mesh axis runs over, the one named last changes fastest.
Arguments:
- velocity: bfloat16 [3, 512, 1024], P(None, 'wide', 'narrow'), may hold values from -6 to 6
- cotangent: bfloat16 [3, 512, 1024], P(None, 'wide', 'narrow'), may hold values from -6 to 6
- kernel_one: bfloat16 [27, 16, 3], replicated, may hold values from -0.625 to 0.625
- kernel_two: bfloat16 [27, 32, 16], replicated, may hold values from -0.3125 to 0.3125
- kernel_three: bfloat16 [27, 64, 32], replicated, may hold values from -0.21875 to 0.21875
- kernel_four: bfloat16 [27, 128, 64], replicated, may hold values from -0.15625 to 0.15625
- lift_four: bfloat16 [64, 128], replicated, may hold values from -0.5 to 0.5
- lift_three: bfloat16 [32, 64], replicated, may hold values from -0.75 to 0.75
- lift_two: bfloat16 [16, 32], replicated, may hold values from -1 to 1
- head: bfloat16 [3, 16], replicated, may hold values from -1.5 to 1.5
Outputs:
- prediction: float32 [3, 512, 1024], P(None, 'wide', 'narrow')
- grad_velocity: float32 [3, 512, 1024], P(None, 'wide', 'narrow')
- grad_kernel_one: float32 [27, 16, 3], replicated
- grad_kernel_two: float32 [27, 32, 16], replicated
- grad_kernel_three: float32 [27, 64, 32], replicated
- grad_kernel_four: float32 [27, 128, 64], replicated
- grad_lift_four: float32 [64, 128], replicated
- grad_lift_three: float32 [32, 64], replicated
- grad_lift_two: float32 [16, 32], replicated
- grad_head: float32 [3, 16], replicated
All inputs are finite; a program needn't handle non-finite values.
Results may differ from a plain program's by a relative error of at most 0.012.
The roundings to bfloat16 on the way count: a program that leaves them out, or rounds other values in their place, can miss the bound.
Values may be sent and summed in bfloat16 or wider, within the bound.
No kernel may reach another device: no remote copies, remote signals or barrier semaphores. Data moves between devices by JAX's collectives and lax.ppermute only.
A program may use at most 64 MiB of HBM per device.

v0:
```python
import jax
import jax.numpy as jnp
import numpy as np
from jax import lax
from jax.sharding import PartitionSpec as P

NZ = 16


def with_halo(block, sides, width):
    for axis, dim in sides:
        count = lax.axis_size(axis)
        forward = [(i, i + 1) for i in range(count - 1)]
        forward.append((count - 1, 0))
        backward = [(target, source) for source, target in forward]
        low = lax.ppermute(
            lax.slice_in_dim(block, block.shape[dim] - width, None, axis=dim), axis, forward
        )
        high = lax.ppermute(lax.slice_in_dim(block, 0, width, axis=dim), axis, backward)
        block = jnp.concatenate([low, block, high], axis=dim)
    return block


def silu_slope(pre):
    sigma = jax.nn.sigmoid(pre)
    return sigma * (1.0 + pre * (1.0 - sigma))


def patch_table(source, lead, wraps, extent):
    coords = np.meshgrid(
        np.arange(extent[0]), np.arange(extent[1]), np.arange(extent[2]), indexing="ij"
    )
    outside = source[0] * source[1] * source[2]
    tables = []
    for offset in range(27):
        moves = (offset // 9, offset // 3 % 3, offset % 3)
        position = np.zeros(tuple(extent), np.int64)
        inside = np.ones(tuple(extent), bool)
        for along in range(3):
            spot = coords[along] + moves[along] - 1 + lead[along]
            if wraps[along]:
                spot = spot % source[along]
            inside = inside & (spot >= 0) & (spot < source[along])
            spot = np.clip(spot, 0, source[along] - 1)
            position = position * source[along] + spot
        tables.append(np.where(inside, position, outside).reshape(-1))
    return np.concatenate(tables).astype(np.int32)


def pool_table(extent):
    half = (extent[0] // 2, extent[1] // 2, extent[2] // 2)
    coords = np.meshgrid(np.arange(half[0]), np.arange(half[1]), np.arange(half[2]), indexing="ij")
    tables = []
    for corner in range(8):
        first, second, third = (corner // 4, corner // 2 % 2, corner % 2)
        position = (
            ((2 * coords[0] + first) * extent[1] + 2 * coords[1] + second) * extent[2]
            + 2 * coords[2]
            + third
        )
        tables.append(position.reshape(-1))
    return np.concatenate(tables).astype(np.int32)


def enlarge_table(coarse):
    coords = np.meshgrid(
        np.arange(2 * coarse[0]), np.arange(2 * coarse[1]), np.arange(2 * coarse[2]), indexing="ij"
    )
    position = (coords[0] // 2 * coarse[1] + coords[1] // 2) * coarse[2] + coords[2] // 2
    return position.reshape(-1).astype(np.int32)


def unfold(source, table):
    chans = source.shape[0]
    extended = jnp.concatenate([source, jnp.zeros((chans, 1), source.dtype)], axis=1)
    picked = jnp.take(extended, jnp.asarray(table), axis=1)
    return picked.reshape(chans * 27, -1)


def correlate(columns, kernel):
    matrix = jnp.transpose(kernel, (1, 2, 0)).reshape(kernel.shape[1], -1)
    return jnp.dot(matrix, columns, preferred_element_type=jnp.float32)


def kernel_slope(columns, delta):
    product = lax.dot_general(
        delta, columns, (((1,), (1,)), ((), ())), preferred_element_type=jnp.float32
    )
    return jnp.transpose(product.reshape(delta.shape[0], -1, 27), (2, 0, 1))


def reflect(kernel):
    return jnp.transpose(kernel[::-1], (0, 2, 1))


def cells_dot(left, right):
    return lax.dot_general(
        left, right, (((1,), (1,)), ((), ())), preferred_element_type=jnp.float32
    )


def pool_sum(field, extent):
    picked = jnp.take(field, jnp.asarray(pool_table(extent)), axis=1).astype(jnp.float32)
    return picked.reshape(field.shape[0], 8, -1).sum(axis=1)


def shrink(field, extent):
    return (pool_sum(field, extent) * 0.125).astype(jnp.bfloat16)


def enlarge(field, coarse):
    return jnp.take(field, jnp.asarray(enlarge_table(coarse)), axis=1)


def project(weight, field):
    return jnp.dot(weight, field, preferred_element_type=jnp.float32)


def fine_unfold(field, extent):
    grown = with_halo(
        field.reshape(field.shape[0], extent[0], extent[1], extent[2]),
        (("wide", 1), ("narrow", 2)),
        1,
    )
    table = patch_table(
        (extent[0] + 2, extent[1] + 2, extent[2]), (1, 1, 0), (False, False, False), extent
    )
    return unfold(grown.reshape(field.shape[0], -1), table)


def mid_unfold(field, extent):
    grown = with_halo(
        field.reshape(field.shape[0], extent[0], extent[1], extent[2]),
        (("wide", 1), ("narrow", 2)),
        1,
    )
    table = patch_table(
        (extent[0] + 2, extent[1] + 2, extent[2]), (1, 1, 0), (False, False, False), extent
    )
    return unfold(grown.reshape(field.shape[0], -1), table)


def coarse_unfold(field, extent):
    grown = with_halo(field.reshape(field.shape[0], extent[0], -1), (("wide", 1),), 1)
    table = patch_table(
        (extent[0] + 2, extent[1], extent[2]), (1, 0, 0), (False, True, False), extent
    )
    return unfold(grown.reshape(field.shape[0], -1), table)


def slice_rows(field, extent, start, count):
    view = field.reshape(field.shape[0], extent[0], -1)
    piece = lax.dynamic_slice_in_dim(view, start * extent[2], count * extent[2], 2)
    return piece.reshape(field.shape[0], -1)


def slice_cols(field, extent, start, count):
    view = field.reshape(field.shape[0], extent[0], -1)
    piece = lax.dynamic_slice_in_dim(view, start, count, 1)
    return piece.reshape(field.shape[0], -1)


def local(
    velocity,
    cotangent,
    kernel_one,
    kernel_two,
    kernel_three,
    kernel_four,
    lift_four,
    lift_three,
    lift_two,
    head,
):
    wide_count = lax.axis_size("wide")
    narrow_count = lax.axis_size("narrow")
    wide_index = lax.axis_index("wide")
    narrow_index = lax.axis_index("narrow")
    chans, cols_x, flat_cells = velocity.shape
    depth = NZ
    rows_y = flat_cells // depth
    extent_fine = (cols_x, rows_y, depth)
    extent_mid = (cols_x // 2, rows_y // 2, depth // 2)
    part_y = rows_y // 4
    extent_part = (cols_x // 4, part_y, depth // 4)
    extent_coarse = (cols_x // 4, part_y * narrow_count, depth // 4)
    tile_x = cols_x // 8
    extent_tile = (tile_x, extent_coarse[1] // 2, depth // 8)
    extent_whole = (tile_x * wide_count, extent_coarse[1] // 2, depth // 8)
    own_y = narrow_index * part_y
    field = velocity.reshape(chans, -1)
    cols_fine = fine_unfold(field, extent_fine)
    pre_fine = correlate(cols_fine, kernel_one)
    act_fine = jax.nn.silu(pre_fine).astype(jnp.bfloat16)
    pooled_mid = shrink(act_fine, extent_fine)
    cols_mid = mid_unfold(pooled_mid, extent_mid)
    pre_mid = correlate(cols_mid, kernel_two)
    act_mid = jax.nn.silu(pre_mid).astype(jnp.bfloat16)
    part_coarse = shrink(act_mid, extent_mid)
    gathered_coarse = lax.all_gather(
        part_coarse.reshape(part_coarse.shape[0], extent_part[0], -1), "narrow", axis=2, tiled=True
    )
    pooled_coarse = gathered_coarse.reshape(part_coarse.shape[0], -1)
    cols_coarse = coarse_unfold(pooled_coarse, extent_coarse)
    pre_coarse = correlate(cols_coarse, kernel_three)
    act_coarse = jax.nn.silu(pre_coarse).astype(jnp.bfloat16)
    width_three = act_coarse.shape[0]
    small = shrink(act_coarse, extent_coarse)
    pooled_bottom = lax.all_gather(
        small.reshape(width_three, tile_x, -1), "wide", axis=1, tiled=True
    ).reshape(width_three, -1)
    bottom_table = patch_table(extent_whole, (0, 0, 0), (True, True, False), extent_whole)
    cols_bottom = unfold(pooled_bottom, bottom_table)
    pre_bottom = correlate(cols_bottom, kernel_four)
    act_bottom = jax.nn.silu(pre_bottom).astype(jnp.bfloat16)
    bottom_x = wide_index * tile_x
    own_bottom = slice_cols(act_bottom, extent_whole, bottom_x, tile_x)
    skip_coarse = (act_coarse + enlarge(project(lift_four, own_bottom), extent_tile)).astype(
        jnp.bfloat16
    )
    skip_part = slice_rows(skip_coarse, extent_coarse, own_y, part_y)
    skip_mid = (act_mid + enlarge(project(lift_three, skip_part), extent_part)).astype(jnp.bfloat16)
    skip_fine = (act_fine + enlarge(project(lift_two, skip_mid), extent_mid)).astype(jnp.bfloat16)
    prediction = project(head, skip_fine)
    incoming = cotangent.reshape(chans, -1)
    grad_head = cells_dot(incoming, skip_fine)
    back_fine = project(head.T, incoming).astype(jnp.bfloat16)
    carry_mid = pool_sum(back_fine, extent_fine).astype(jnp.bfloat16)
    grad_lift_two = cells_dot(carry_mid, skip_mid)
    back_mid = project(lift_two.T, carry_mid).astype(jnp.bfloat16)
    carry_coarse = pool_sum(back_mid, extent_mid).astype(jnp.bfloat16)
    grad_lift_three = cells_dot(carry_coarse, skip_part)
    back_part = project(lift_three.T, carry_coarse).astype(jnp.bfloat16)
    back_coarse = lax.all_gather(
        back_part.reshape(width_three, extent_part[0], -1), "narrow", axis=2, tiled=True
    ).reshape(width_three, -1)
    carry_own = pool_sum(back_part, extent_part).astype(jnp.bfloat16)
    half_part = part_y // 2
    own_act = slice_rows(own_bottom, extent_tile, narrow_index * half_part, half_part)
    grad_lift_four = cells_dot(carry_own, own_act)
    carry_tile = pool_sum(back_coarse, extent_coarse).astype(jnp.bfloat16)
    carry_bottom = lax.all_gather(
        carry_tile.reshape(width_three, tile_x, -1), "wide", axis=1, tiled=True
    ).reshape(width_three, -1)
    slope_bottom = project(lift_four.T, carry_bottom)
    delta_bottom = (slope_bottom * silu_slope(pre_bottom)).astype(jnp.bfloat16)
    grad_kernel_four = kernel_slope(cols_bottom, delta_bottom)
    return_bottom = correlate(unfold(delta_bottom, bottom_table), reflect(kernel_four))
    return_tile = slice_cols(return_bottom, extent_whole, bottom_x, tile_x)
    slope_coarse = back_coarse + enlarge(return_tile, extent_tile) * 0.125
    delta_coarse = (slope_coarse * silu_slope(pre_coarse)).astype(jnp.bfloat16)
    cols_part = slice_rows(cols_coarse, extent_coarse, own_y, part_y)
    delta_part = slice_rows(delta_coarse, extent_coarse, own_y, part_y)
    grad_kernel_three = kernel_slope(cols_part, delta_part)
    return_full = correlate(coarse_unfold(delta_coarse, extent_coarse), reflect(kernel_three))
    return_coarse = slice_rows(return_full, extent_coarse, own_y, part_y)
    slope_mid = back_mid + enlarge(return_coarse, extent_part) * 0.125
    delta_mid = (slope_mid * silu_slope(pre_mid)).astype(jnp.bfloat16)
    grad_kernel_two = kernel_slope(cols_mid, delta_mid)
    return_mid = correlate(mid_unfold(delta_mid, extent_mid), reflect(kernel_two))
    slope_fine = back_fine + enlarge(return_mid, extent_mid) * 0.125
    delta_fine = (slope_fine * silu_slope(pre_fine)).astype(jnp.bfloat16)
    grad_kernel_one = kernel_slope(cols_fine, delta_fine)
    grad_velocity = correlate(fine_unfold(delta_fine, extent_fine), reflect(kernel_one))
    (
        grad_head,
        grad_lift_two,
        grad_lift_three,
        grad_lift_four,
        grad_kernel_one,
        grad_kernel_two,
        grad_kernel_three,
    ) = lax.psum(
        (
            grad_head,
            grad_lift_two,
            grad_lift_three,
            grad_lift_four,
            grad_kernel_one,
            grad_kernel_two,
            grad_kernel_three,
        ),
        ("wide", "narrow"),
    )
    scale = float(cols_x * rows_y * depth * wide_count * narrow_count) ** (-0.5)
    return (
        prediction.reshape(chans, cols_x, rows_y * depth),
        grad_velocity.reshape(chans, cols_x, rows_y * depth),
        grad_kernel_one * scale,
        grad_kernel_two * scale,
        grad_kernel_three * scale,
        grad_kernel_four * scale,
        grad_lift_four * scale,
        grad_lift_three * scale,
        grad_lift_two * scale,
        grad_head * scale,
    )


def solution(mesh):
    return jax.shard_map(
        local,
        mesh=mesh,
        in_specs=(
            P(None, "wide", "narrow"),
            P(None, "wide", "narrow"),
            P(),
            P(),
            P(),
            P(),
            P(),
            P(),
            P(),
            P(),
        ),
        out_specs=(
            P(None, "wide", "narrow"),
            P(None, "wide", "narrow"),
            P(),
            P(),
            P(),
            P(),
            P(),
            P(),
            P(),
            P(),
        ),
        check_vma=False,
    )
```

profile of v0, /device:TPU:1, one launch (start us, length us, event | category | flops | bytes accessed | tf_op | source)
XLA Modules:
  0.0 1126.6 jit_solution(9987310099263943480)
XLA Ops:
  8.0 14.4 %collective-permute-start.1 = (bf16[3,1,8,16]{3,2,1,0:T(8,128)(2,1)S(1)}, bf16[3,1,8,16]{3,2,1,0:T(8,128)(2,1)S(1)}, u32[]{:S(2)}, u32[]{:S(2)}) collective-permute-start(bf16[3,1,8,16]{3,2,1,0:T(8,128)(2,1)S(1)} %get-tuple-element.72), channel_id=1, source_target_pairs={{8,0},{16,8},{24,16},{32,24},{40,32},{48,40},{56,48},{64,56},{72,6... | collective-permute-start | bytes 2312 | tf_op jit(solution)/shard_map/ppermute | solution.py:19
  41.5 96.4 %gather_fusion = bf16[27648,3]{1,0:T(8,128)(2,1)} fusion(bf16[3,1601]{0,1:T(8,128)(2,1)S(1)} %concatenate.56, s32[27648]{0:T(1024)S(1)} %broadcast_clamp_fusion.1), kind=kCustom, calls=%fused_computation.12 | custom fusion | bytes 442368 | tf_op jit(solution)/shard_map/jit(_take)/gather | solution.py:76
  137.9 6.8 copy.167
  151.0 7.0 collective-permute-start.5
  159.8 15.5 %all_gather.14 = bf16[64,2,64]{0,1,2:T(2,128)(2,1)S(1)} all-gather(bf16[64,2,8]{0,1,2:T(2,128)(2,1)S(1)} %copy.181), channel_id=1, replica_groups=mesh['wide'=64,'narrow'=8] {'narrow'}, dimensions={2}, use_global_device_ids=true | all-gather | bytes 18432 | tf_op jit(solution)/shard_map/all_gather | solution.py:234
  176.5 7.1 gather_fusion.1
  185.0 11.2 all_gather.12
  198.1 7.2 collective-permute-start.9
  205.4 37.8 %all-gather.1 = bf16[64,1024]{0,1:T(8,128)(2,1)} all-gather(bf16[64,16]{0,1:T(8,128)(2,1)S(1)} %reduce.3), channel_id=3, replica_groups=mesh['wide'=64,'narrow'=8] {'wide'}, dimensions={1}, use_global_device_ids=true | all-gather | bytes 133120 | tf_op jit(solution)/shard_map/all_gather | solution.py:242
  245.1 7.1 gather_fusion.2
  253.6 37.7 %all-gather = bf16[64,1024]{0,1:T(8,128)(2,1)S(1)} all-gather(bf16[64,16]{0,1:T(8,128)(2,1)S(1)} %multiply_convert_fusion.5), channel_id=2, replica_groups=mesh['wide'=64,'narrow'=8] {'wide'}, dimensions={1}, use_global_device_ids=true | all-gather | bytes 133120 | tf_op jit(solution)/shard_map/all_gather | solution.py:209
  291.4 96.4 %gather_fusion.3 = bf16[27648,64]{1,0:T(8,128)(2,1)} fusion(bf16[64,1025]{0,1:T(8,128)(2,1)S(1)} %concatenate.62, s32[27648]{0:T(1024)S(1)} %broadcast_clamp_fusion), kind=kCustom, calls=%fused_computation.15 | custom fusion | bytes 7188480 | tf_op jit(solution)/shard_map/jit(_take)/gather | solution.py:76
  399.1 96.4 %gather_fusion.4 = bf16[27648,128]{1,0:T(8,128)(2,1)} fusion(bf16[128,1025]{0,1:T(8,128)(2,1)S(1)} %concatenate.63, s32[27648]{0:T(1024)S(1)} %broadcast_clamp_fusion), kind=kCustom, calls=%fused_computation.16 | custom fusion | bytes 14266368 | tf_op jit(solution)/shard_map/jit(_take)/gather | solution.py:76
  495.5 5.3 convolution_bitcast_fusion.4
  510.3 6.7 collective-permute-start.11
  519.8 7.1 gather_fusion.5
  530.5 6.7 collective-permute-start.13
  538.0 25.5 %collective-permute-start.14 = (bf16[32,6,1,8]{0,3,2,1:T(8,128)(2,1)S(1)}, bf16[32,6,1,8]{0,3,2,1:T(8,128)(2,1)S(1)}, u32[]{:S(2)}, u32[]{:S(2)}) collective-permute-start(bf16[32,6,1,8]{0,3,2,1:T(8,128)(2,1)S(1)} %get-tuple-element.68), channel_id=1, source_target_pairs={{0,1},{1,2},{2,3},{3,4},{4,5},{5,6},{6,7},{7,0},{8,9},{9,10},{10,1... | collective-permute-start | bytes 9224 | tf_op jit(solution)/shard_map/ppermute | solution.py:16
  566.7 7.1 gather_fusion.6
  580.4 7.2 collective-permute-start.17
  594.7 96.4 %gather_fusion.7 = bf16[27648,16]{1,0:T(8,128)(2,1)} fusion(bf16[16,1601]{0,1:T(8,128)(2,1)S(1)} %concatenate.71, s32[27648]{0:T(1024)S(1)} %broadcast_clamp_fusion.1), kind=kCustom, calls=%fused_computation.19 | custom fusion | bytes 1880064 | tf_op jit(solution)/shard_map/jit(_take)/gather | solution.py:76
  691.1 4.9 convolution_bitcast_fusion.9
  696.7 153.0 %all-reduce.14.cloned.1.call-done = (f32[27,16,3]{0,1,2:T(8,128)}, f32[27,32,16]{0,1,2:T(8,128)}, f32[64,128]{1,0:T(8,128)}, f32[32,64]{1,0:T(8,128)}, f32[16,32]{1,0:T(8,128)}, /*index=5*/f32[3,16]{1,0:T(4,128)}) async-done(((f32[27,16,3]{0,1,2:T(8,128)}, f32[27,32,16]{0,1,2:T(8,128)}, f32[64,128]{1,0:T(8,128)}, f32[32,64]{1,0:T(8,128)}, f32[16,32]{1,0:T(8,128)}, /*index=5*/f32[3,16]{1,0:T(4,128)}), ...) | async-done | bytes 103696 | tf_op jit(solution)/shard_map/psum | solution.py:273
  858.1 259.9 %all-reduce.12.cloned.1.call-done = f32[27,64,32]{1,2,0:T(8,128)} async-done(((f32[27,64,32]{1,2,0:T(8,128)}), f32[27,64,32]{1,2,0:T(8,128)}) %all-reduce.12.cloned.1.call-update) | async-done | bytes 221200 | tf_op jit(solution)/shard_map/psum | solution.py:273
  (209 shorter events, 90.6 us)
Async XLA Ops:
  7.2 385.3 %copy-start = (bf16[64,128]{1,0:T(8,128)(2,1)S(1)}, bf16[64,128]{1,0:T(8,128)(2,1)}, u32[]{:S(2)}) copy-start(bf16[64,128]{1,0:T(8,128)(2,1)} %param.48) | copy-start | bytes 49156
  7.2 842.5 %all-reduce.14.cloned.1.call-start = ((), (), s32[]{:S(2)}) async-start(), calls=%async_computation.1 | async-start | bytes 692224 | tf_op jit(solution)/shard_map/psum | solution.py:273
  8.0 27.3 %collective-permute-start.1 = (bf16[3,1,8,16]{3,2,1,0:T(8,128)(2,1)S(1)}, bf16[3,1,8,16]{3,2,1,0:T(8,128)(2,1)S(1)}, u32[]{:S(2)}, u32[]{:S(2)}) collective-permute-start(bf16[3,1,8,16]{3,2,1,0:T(8,128)(2,1)S(1)} %get-tuple-element.72), channel_id=1, source_target_pairs={{8,0},{16,8},{24,16},{32,24},{40,32},{48,40},{56,48},{64,56},{72,6... | collective-permute-start | bytes 2312 | tf_op jit(solution)/shard_map/ppermute | solution.py:19
  22.5 12.9 %collective-permute-start = (bf16[3,1,8,16]{3,2,1,0:T(8,128)(2,1)S(1)}, bf16[3,1,8,16]{3,2,1,0:T(8,128)(2,1)S(1)}, u32[]{:S(2)}, u32[]{:S(2)}) collective-permute-start(bf16[3,1,8,16]{3,2,1,0:T(8,128)(2,1)S(1)} %get-tuple-element.73), channel_id=1, source_target_pairs={{0,8},{8,16},{16,24},{24,32},{32,40},{40,48},{48,56},{56,64},{64,7... | collective-permute-start | bytes 2312 | tf_op jit(solution)/shard_map/ppermute | solution.py:16
  35.4 3.3 collective-permute-start.2
  37.5 3.2 collective-permute-start.3
  41.5 203.1 %copy-start.3 = (bf16[27,128,64]{1,2,0:T(8,128)(2,1)S(1)}, bf16[27,128,64]{1,2,0:T(8,128)(2,1)}, u32[]{:S(2)}) copy-start(bf16[27,128,64]{1,2,0:T(8,128)(2,1)} %param.47) | copy-start | bytes 1327108
  149.1 9.5 collective-permute-start.4
  151.0 7.7 collective-permute-start.5
  158.8 17.6 %collective-permute-start.6 = (bf16[16,6,1,8]{0,3,2,1:T(8,128)(2,1)S(1)}, bf16[16,6,1,8]{0,3,2,1:T(8,128)(2,1)S(1)}, u32[]{:S(2)}, u32[]{:S(2)}) collective-permute-start(bf16[16,6,1,8]{0,3,2,1:T(8,128)(2,1)S(1)} %get-tuple-element.70), channel_id=1, source_target_pairs={{0,1},{1,2},{2,3},{3,4},{4,5},{5,6},{6,7},{7,0},{8,9},{9,10},{10,1... | collective-permute-start | bytes 4616 | tf_op jit(solution)/shard_map/ppermute | solution.py:16
  159.7 16.8 %collective-permute-start.7 = (bf16[16,6,1,8]{0,3,2,1:T(8,128)(2,1)S(1)}, bf16[16,6,1,8]{0,3,2,1:T(8,128)(2,1)S(1)}, u32[]{:S(2)}, u32[]{:S(2)}) collective-permute-start(bf16[16,6,1,8]{0,3,2,1:T(8,128)(2,1)S(1)} %get-tuple-element.71), channel_id=1, source_target_pairs={{1,0},{2,1},{3,2},{4,3},{5,4},{6,5},{7,6},{0,7},{9,8},{10,9},{11,1... | collective-permute-start | bytes 4616 | tf_op jit(solution)/shard_map/ppermute | solution.py:19
  196.2 48.8 %collective-permute-start.8 = (bf16[32,1,64]{0,2,1:T(8,128)(2,1)S(1)}, bf16[32,1,64]{0,2,1:T(8,128)(2,1)S(1)}, u32[]{:S(2)}, u32[]{:S(2)}) collective-permute-start(bf16[32,1,64]{0,2,1:T(8,128)(2,1)S(1)} %get-tuple-element.78), channel_id=1, source_target_pairs={{0,8},{8,16},{16,24},{24,32},{32,40},{40,48},{48,56},{56,64},{64,7... | collective-permute-start | bytes 12296 | tf_op jit(solution)/shard_map/ppermute | solution.py:16
  198.1 46.9 %collective-permute-start.9 = (bf16[32,1,64]{0,2,1:T(8,128)(2,1)S(1)}, bf16[32,1,64]{0,2,1:T(8,128)(2,1)S(1)}, u32[]{:S(2)}, u32[]{:S(2)}) collective-permute-start(bf16[32,1,64]{0,2,1:T(8,128)(2,1)S(1)} %get-tuple-element.79), channel_id=1, source_target_pairs={{8,0},{16,8},{24,16},{32,24},{40,32},{48,40},{56,48},{64,56},{72,6... | collective-permute-start | bytes 12296 | tf_op jit(solution)/shard_map/ppermute | solution.py:19
  508.4 11.1 collective-permute-start.10
  510.3 9.2 collective-permute-start.11
  528.6 9.4 collective-permute-start.12
  530.5 7.5 collective-permute-start.13
  538.0 27.2 %collective-permute-start.14 = (bf16[32,6,1,8]{0,3,2,1:T(8,128)(2,1)S(1)}, bf16[32,6,1,8]{0,3,2,1:T(8,128)(2,1)S(1)}, u32[]{:S(2)}, u32[]{:S(2)}) collective-permute-start(bf16[32,6,1,8]{0,3,2,1:T(8,128)(2,1)S(1)} %get-tuple-element.68), channel_id=1, source_target_pairs={{0,1},{1,2},{2,3},{3,4},{4,5},{5,6},{6,7},{7,0},{8,9},{9,10},{10,1... | collective-permute-start | bytes 9224 | tf_op jit(solution)/shard_map/ppermute | solution.py:16
  563.6 3.1 collective-permute-start.15
  577.6 10.3 collective-permute-start.16
  580.4 8.2 collective-permute-start.17
  587.6 530.3 %all-reduce.12.cloned.1.call-start = ((), (), s32[]{:S(2)}) async-start(), calls=%async_computation | async-start | bytes 884736 | tf_op jit(solution)/shard_map/psum | solution.py:273
  588.8 3.5 collective-permute-start.18
  589.8 3.9 collective-permute-start.19
  (14 other events, 963.9 us)
Sparse Core Ops, SparseCore 0:
  587.8 261.8 all-reduce.13
  856.0 261.9 all-reduce.11
where the time goes:
time: 1130 us
  local copies, waits for them, and re-layouts  451 us (40%)
  waiting for transfers between devices  419 us (37%)
  blocking collectives  102 us (9%)
  starting transfers between devices  92.9 us (8%)
  matrix products  30.4 us (3%)
  other arithmetic  16.9 us (1%)
  between operations  14.9 us (1%)
    gather x12, local copies, waits for them, and re-layouts, unfold(): picked = jnp.take(extended, jnp.asarray(table), axis=1)  422 us
    psum x2, waiting for transfers between devices, local(): lax.psum((grad_head, grad_lift_two, grad_lift_three, grad_lift_four, grad...  413 us
    ppermute x10, starting transfers between devices, with_halo(): lax.ppermute(lax.slice_in_dim(block, 0, width, axis=dim), axis, backward)  51.6 us
    ppermute x10, starting transfers between devices, with_halo(): lax.ppermute(lax.slice_in_dim(block, block.shape[dim] - width, None, axis...  41.1 us
    all_gather x1, blocking collectives, local(): lax.all_gather(carry_tile.reshape(width_three, tile_x, -1), 'wide', axis=...  37.8 us
    all_gather x1, blocking collectives, local(): lax.all_gather(small.reshape(width_three, tile_x, -1), 'wide', axis=1, ti...  37.7 us
  transfers between devices with their start and end apart: 22, of which 7 were waited for; matrix products, arithmetic and copies ran while one was open for 12% of the time, Pallas kernels for 0%

commit v1 on v0

v1 whole, which is shorter than its diff:
```python
import jax
import jax.numpy as jnp
import numpy as np
from jax import lax
from jax.experimental import pallas as pl
from jax.experimental.pallas import tpu as pltpu
from jax.sharding import PartitionSpec as P

BF = jnp.bfloat16
F32 = jnp.float32
NZ = 16
LINES = 9
PIECE = 40
SHARE = 8 * PIECE
PACK = 8 * SHARE


def mm(a, b):
    return lax.dot_general(a, b, (((1,), (0,)), ((), ())), preferred_element_type=F32)


def mm_nt(a, b):
    return lax.dot_general(a, b, (((1,), (1,)), ((), ())), preferred_element_type=F32)


def mm_tn(a, b):
    return lax.dot_general(a, b, (((0,), (0,)), ((), ())), preferred_element_type=F32)


def halves(x):
    high = x.astype(BF)
    return high, (x - high.astype(F32)).astype(BF)


def mm2(x, e):
    high, low = halves(x)
    return mm(high, e) + mm(low, e)


def iota(shape, axis):
    return lax.broadcasted_iota(jnp.int32, shape, axis)


def log2(n):
    return int(n).bit_length() - 1


def one_hot(mask):
    return jnp.where(mask, 1.0, 0.0).astype(BF)


def pool_matrix(chans):
    row, col = iota((256, 128), 0), iota((256, 128), 1)
    shift = log2(chans)
    same = (row & (chans - 1)) == (col & (chans - 1))
    return one_hot(same & ((row >> (shift + 1)) == (col >> shift)))


def tile_matrix(chans, lanes):
    return one_hot(iota((chans, lanes), 0) == (iota((chans, lanes), 1) & (chans - 1)))


def fold_matrix(rows, chans, lead):
    row, col = iota((rows, 128), 0), iota((rows, 128), 1)
    return one_hot((row & (chans - 1)) + lead == col)


def shift_y(v, count, step):
    rows = v.shape[0]
    out = pltpu.roll(v, (-step) % rows, 0)
    if rows == count:
        return out
    if step == 1:
        other, edge = pltpu.roll(v, count - 1, 0), count - 1
    else:
        other, edge = pltpu.roll(v, rows - (count - 1), 0), 0
    spot = iota(v.shape, 0) & (count - 1)
    return jnp.where(spot == edge, other, out)


def silu_of(pre):
    half = 0.5 * pre
    return half + half * jnp.tanh(half)


def slope_of(pre):
    half = 0.5 * pre
    bend = jnp.tanh(half)
    return (0.5 + 0.5 * bend) * (1.0 + half * (1.0 - bend))


def prep_kernel(vel_ref, cot_ref, place_ref, out_ref):
    row, col = iota((64, 128), 0), iota((64, 128), 1)
    mask = (row & 7) == (col >> 4)
    spread = one_hot((iota((64, 8), 0) >> 3) == iota((64, 8), 1))
    total = jnp.zeros((64, 128), F32)
    for part, ref in ((0, vel_ref), (1, cot_ref)):
        for chan in range(3):
            wide = mm(spread, ref[chan])
            kept = jnp.where(mask, wide, 0.0).astype(BF)
            total = total + mm(kept, place_ref[part * 3 + chan])
    last = total[48:64]
    spare = iota((16, 128), 1) >= 96
    for g in range(3):
        moved = pltpu.roll(last, 96 - 32 * g, 1)
        out_ref[g * 16:(g + 1) * 16, :] = jnp.where(
            spare, moved, total[g * 16:(g + 1) * 16]
        ).astype(BF)


def build_kernel(
    k1_ref,
    k2_ref,
    k3_ref,
    k4_ref,
    l4_ref,
    l3_ref,
    l2_ref,
    head_ref,
    band_ref,
    base_ref,
    rowrep_ref,
    headmask_ref,
    t1,
    t2,
    t3,
    t4,
    f4,
    f3,
    f2,
    hp,
    b4,
    b3,
    b2,
    small,
):
    def build(kernel_ref, t_ref, outs, ins):
        planes = 128 // ins
        rep = mm(kernel_ref[...], tile_matrix(outs, 256))
        kout = iota((ins, 256), 1) >> log2(outs)
        for ab in range(9):
            a, b = ab // 3, ab % 3
            taps = [rep[(ab * 3 + c) * ins:(ab * 3 + c + 1) * ins] for c in range(3)]
            for k in range(planes):
                block = jnp.zeros((ins, 256), F32)
                for c in range(3):
                    if 0 <= k - c + 1 < planes:
                        block = jnp.where(kout == k - c + 1, taps[c], block)
                start = b * 128 + k * ins
                t_ref[a, start:start + ins, :] = block.astype(BF)

    build(k2_ref, t2, 32, 16)
    build(k3_ref, t3, 64, 32)
    build(k4_ref, t4, 128, 64)
    small[...] = jnp.zeros(small.shape, F32)
    for c in range(3):
        small[c * 32:c * 32 + 27, :] = mm_tn(k1_ref[c], tile_matrix(16, 256))
    rep1 = small[...].astype(BF)
    base = base_ref[...]
    band = band_ref[...]
    for a in range(3):
        block = jnp.zeros((256, 256), F32)
        for c in range(3):
            block = jnp.where(band == c, mm(one_hot(base == 9 * a + c), rep1), block)
        t1[a] = block.astype(BF)

    def lift(lift_ref, f_ref, b_ref, coarse):
        fine, chans = lift_ref.shape
        rep = mm(lift_ref[...], tile_matrix(chans, 256))
        kin = iota((fine, 256), 1) >> log2(chans)
        for k in range(2 * coarse):
            f_ref[k * fine:(k + 1) * fine, :] = jnp.where(kin == k // 2, rep, 0.0).astype(BF)
        for k in range(coarse):
            b_ref[k * fine:(k + 1) * fine, :] = jnp.where(kin == k, rep, 0.0).astype(BF)

    lift(l4_ref, f4, b4, 2)
    lift(l3_ref, f3, b3, 4)
    lift(l2_ref, f2, b2, 8)
    small[0:16, 0:128] = jnp.zeros((16, 128), F32)
    small[0:3, 0:16] = head_ref[...].astype(F32)
    tileh = one_hot(iota((128, 256), 0) == (iota((128, 256), 1) & 15))
    reph = mm(small[0:16, 0:128].astype(BF), tileh).astype(BF)
    hp[...] = (mm(rowrep_ref[...], reph) * headmask_ref[...]).astype(BF)


def main_kernel(
    where_ref,
    own_ref,
    tiles_ref,
    t1,
    t2,
    t3,
    t4,
    f4,
    f3,
    f2,
    hp,
    b4,
    b3,
    b2,
    band_ref,
    pick_ref,
    rowrep_ref,
    headmask_ref,
    unplace_ref,
    pred_ref,
    gradv_ref,
    share_ref,
    xt,
    xc,
    v3,
    pre1,
    act1,
    pre2,
    act2,
    pre3,
    act3,
    p32,
    p33,
    p34,
    skip1,
    carry2,
    carry3,
    back2,
    back3,
    d1,
    d2,
    d3,
    d4,
    ret2,
    tmp,
    ups_a,
    ups_b,
    line,
    pack,
):
    own_part = where_ref[0]
    lane = iota((1, 128), 1)
    band = band_ref[...]

    pool1, pool2, pool3 = pool_matrix(16), pool_matrix(32), pool_matrix(64)

    def rows(start, count, unit):
        return pl.ds(pl.multiple_of(start, unit), count)

    v3[0:64, :] = jnp.zeros((64, 256), BF)
    v3[73 * 64:74 * 64, :] = jnp.zeros((64, 256), BF)

    def arrange(source, number):
        for n in range(8):
            tile = source(n).astype(F32)
            last = jnp.zeros((16, 128), F32)
            for g in range(3):
                moved = pltpu.roll(tile[g * 16:(g + 1) * 16], 32 * (g + 1), 1)
                last = jnp.where((lane >= 32 * g) & (lane < 32 * g + 32), moved, last)
            for i in range(8):
                piece = tile[i * 8:i * 8 + 8] if i < 6 else last[(i - 6) * 8:(i - 5) * 8]
                xt[i * 64 + n * 8:i * 64 + n * 8 + 8, :] = piece
        for i in range(8):
            row = xt[i * 64:(i + 1) * 64, :]
            xc[rows((number * 8 + i) * 64, 64, 64), :] = row.astype(BF)
            vel = jnp.where(lane < 48, row, 0.0)
            low = pltpu.roll(vel, 1, 0) + pltpu.roll(vel, 48, 1)
            high = pltpu.roll(vel, 63, 0)
            spot = rows((number * 8 + i + 1) * 64, 64, 64)
            v3[spot, 0:128] = low.astype(BF)
            v3[spot, 128:256] = high.astype(BF)

    def arrange_far(step, _):
        arrange(lambda n: tiles_ref[step, n], where_ref[1 + step])
        return 0

    arrange(lambda n: own_ref[n], 4)
    lax.fori_loop(0, 8, arrange_far, 0)

    def pooled(field, matrix, count):
        flat = mm(field, matrix)
        pairs = field.shape[0] // (2 * count)
        for i in range(pairs):
            tmp[i * count:(i + 1) * count, :] = (
                flat[2 * i * count:(2 * i + 1) * count] + flat[(2 * i + 1) * count:(2 * i + 2) * count]
            )
        n = pairs * count // 2
        return tmp[pl.ds(0, n, stride=2), :] + tmp[pl.ds(1, n, stride=2), :]

    def enlarged(field, count):
        n = field.shape[0]
        for half, ref in ((0, ups_a), (1, ups_b)):
            piece = field[:, half * 128:(half + 1) * 128]
            ref[pl.ds(0, n, stride=2), :] = piece
            ref[pl.ds(1, n, stride=2), :] = piece
        big = jnp.concatenate([ups_a[0:2 * n, :], ups_b[0:2 * n, :]], axis=1)
        wide = 2 * count
        parts = []
        for i in range(n // count):
            piece = big[i * wide:(i + 1) * wide]
            parts += [piece, piece]
        return jnp.concatenate(parts, axis=0)

    def put3(ref, start, unit, field, count):
        spot = rows(start, field.shape[0], unit)
        kind = ref.dtype
        ref[spot, 0:128] = shift_y(field, count, -1).astype(kind)
        ref[spot, 128:256] = field.astype(kind)
        ref[spot, 256:384] = shift_y(field, count, 1).astype(kind)

    def fine_forward(step, _):
        start = step * 512
        pre = mm(v3[rows(start, 512, 64), :], t1[0])
        for a in (1, 2):
            pre = pre + mm(v3[rows(start + a * 64, 512, 64), :], t1[a])
        pre1[rows(start, 512, 512), :] = pre
        act = silu_of(pre).astype(BF)
        act1[rows(start, 512, 512), :] = act
        half = (pooled(act, pool1, 64) * 0.125).astype(BF).astype(F32)
        put3(p32, step * 128, 32, half, 32)
        return 0

    lax.fori_loop(0, 9, fine_forward, 0)

    def mid_forward(step, _):
        start = (2 + step * 8) * 32
        pre = mm(p32[rows(start - 32, 256, 32), :], t2[0])
        for a in (1, 2):
            pre = pre + mm(p32[rows(start + (a - 1) * 32, 256, 32), :], t2[a])
        pre2[rows(start, 256, 32), :] = pre
        act = silu_of(pre).astype(BF)
        act2[rows(start, 256, 32), :] = act
        half = (pooled(act, pool2, 32) * 0.125).astype(BF).astype(F32)
        put3(p33, (1 + step * 4) * 16, 16, half, 16)
        return 0

    lax.fori_loop(0, 4, mid_forward, 0)

    pre = mm(p33[16:240, :], t3[0])
    for a in (1, 2):
        pre = pre + mm(p33[(1 + a) * 16:(1 + a) * 16 + 224, :], t3[a])
    pre3[...] = pre
    act = silu_of(pre).astype(BF)
    act3[...] = act
    half = (pooled(act, pool3, 16) * 0.125).astype(BF).astype(F32)
    put3(p34, 8, 8, half, 8)

    pre4 = mm(p34[8:48, :].astype(BF), t4[0])
    for a in (1, 2):
        pre4 = pre4 + mm(p34[(1 + a) * 8:(1 + a) * 8 + 40, :].astype(BF), t4[a])
    act4 = silu_of(pre4)[16:24].astype(BF)

    skip3 = (act3[96:128, :].astype(F32) + enlarged(mm_nt(act4, f4[...]), 8)).astype(BF)
    skip2 = (act2[512:640, :].astype(F32) + enlarged(mm_nt(skip3, f3[...]), 16)).astype(BF)
    up2 = mm_nt(skip2, f2[...])
    for half in range(2):
        base = act1[2048 + half * 256:2304 + half * 256, :].astype(F32)
        up = enlarged(up2[half * 64:(half + 1) * 64], 32)
        skip1[half * 256:(half + 1) * 256, :] = (base + up).astype(BF)
    gh = mm_tn(xc[2048:2560, :], skip1[...])

    def fine_carry(step, _):
        back = mm(xc[rows((16 + step * 8) * 64, 512, 512), :], hp[...]).astype(BF)
        carry2[rows((8 + step * 4) * 32, 128, 128), :] = pooled(back, pool1, 64).astype(BF)
        return 0

    lax.fori_loop(0, 5, fine_carry, 0)

    for step in range(5):
        start = (8 + step * 4) * 32
        back = mm(carry2[start:start + 128, :], b2[...]).astype(BF)
        back2[start:start + 128, :] = back
        carry3[step * 32:(step + 1) * 32, :] = pooled(back, pool2, 32).astype(BF)
    back = mm(carry3[...], b3[...]).astype(BF)
    back3[...] = back
    carry4 = pooled(back, pool3, 16)

    gl2 = mm_tn(carry2[512:640, :], skip2)
    gl3 = mm_tn(carry3[64:96, :], skip3)
    gl4 = mm_tn(carry4[16:24].astype(BF), act4)

    delta4 = (mm(carry4.astype(BF), b4[...]) * slope_of(pre4)).astype(BF).astype(F32)
    d4[...] = delta4
    own4 = delta4[16:24].astype(BF)

    def returned(total, count):
        return (
            shift_y(total[:, 0:128], count, 1)
            + total[:, 128:256]
            + shift_y(total[:, 256:384], count, -1)
        )

    total = mm_nt(d4[16:40, :].astype(BF), t4[0])
    for a in (1, 2):
        total = total + mm_nt(d4[(2 - a) * 8:(2 - a) * 8 + 24, :].astype(BF), t4[a])
    ret4 = returned(total, 8)

    def spread_up(field, matrix, count):
        high, low = halves(field * 0.125)
        return enlarged(mm_nt(high, matrix) + mm_nt(low, matrix), count)

    slope = back3[32:128, :].astype(F32) + spread_up(ret4, pool3, 8)
    d3[...] = (slope * slope_of(pre3[64:160, :])).astype(BF)
    total = mm_nt(d3[32:96, :], t3[0])
    for a in (1, 2):
        total = total + mm_nt(d3[(2 - a) * 16:(2 - a) * 16 + 64, :], t3[a])
    ret3 = returned(total, 16)

    slope = back2[14 * 32:22 * 32, :].astype(F32) + spread_up(ret3, pool2, 16)
    d2[...] = (slope * slope_of(pre2[14 * 32:22 * 32, :])).astype(BF)
    total = mm_nt(d2[64:256, :], t2[0])
    for a in (1, 2):
        total = total + mm_nt(d2[(2 - a) * 32:(2 - a) * 32 + 192, :], t2[a])
    ret2[...] = returned(total, 32)

    for step in range(3):
        spot = slice((30 + step * 4) * 64, (34 + step * 4) * 64)
        up = spread_up(ret2[step * 64:(step + 1) * 64, :], pool1, 32)
        back = mm(xc[spot, :], hp[...]).astype(BF).astype(F32)
        d1[step * 256:(step + 1) * 256, :] = ((back + up) * slope_of(pre1[spot, :])).astype(BF)

    guess = mm_nt(skip1[...], hp[...])
    total = mm_nt(d1[192:704, :], t1[0])
    for a in (1, 2):
        total = total + mm_nt(d1[(3 - a) * 64:(3 - a) * 64 + 512, :], t1[a])
    low, high = total[:, 0:128], total[:, 128:256]
    grad = shift_y(low, 64, 1) + pltpu.roll(low, 80, 1) + shift_y(high, 64, -1)
    line[...] = jnp.where(lane < 48, grad, guess)
    pieces = [line[rows(i * 64 + own_part * 8, 8, 8), :] for i in range(8)]
    own = jnp.concatenate(pieces, axis=0)
    first, rest = halves(own)
    second, third = halves(own - first.astype(F32))
    mask = (iota((64, 128), 0) & 7) == (iota((64, 128), 1) >> 4)
    for part, ref in ((0, gradv_ref), (1, pred_ref)):
        for chan in range(3):
            matrix = unplace_ref[part * 3 + chan]
            full = mm(first, matrix) + mm(second, matrix) + mm(third, matrix)
            full = jnp.where(mask, full, 0.0).reshape(8, 8, 128)
            ref[chan] = jnp.sum(full, axis=1)

    pack[1728:PACK, :] = jnp.zeros((PACK - 1728, 128), F32)

    def fold_taps(product, outs, ins, a, b):
        planes = 128 // ins
        kout = iota((ins, 256), 1) >> log2(outs)
        sums = [jnp.zeros((ins, 256), F32) for _ in range(3)]
        for k in range(planes):
            block = product[b * 128 + k * ins:b * 128 + (k + 1) * ins]
            for c in range(3):
                if 0 <= k - c + 1 < planes:
                    sums[c] = sums[c] + jnp.where(kout == k - c + 1, block, 0.0)
        joined = jnp.concatenate(sums, axis=0)
        joined = joined[:, 0:128] + joined[:, 128:256]
        width = outs
        while width < 128:
            joined = joined + pltpu.roll(joined, 128 - width, 1)
            width *= 2
        return joined

    fold4, fold2 = fold_matrix(256, 128, 0), fold_matrix(256, 32, 64)
    for a in range(3):
        product = mm_tn(p34[(3 + a) * 8:(4 + a) * 8, :].astype(BF), own4)
        for b in range(3):
            start = (a * 3 + b) * 192
            pack[start:start + 192, :] = fold_taps(product, 128, 64, a, b)
    for a in range(3):
        product = mm_tn(p33[(7 + a) * 16:(9 + a) * 16, :], d3[32:64, :])
        for b in range(3):
            part = fold_taps(product, 64, 32, a, b)
            left = jnp.where(lane < 64, part, 0.0)
            start = 1728 + (a * 3 + b) * 96
            if a * 3 + b < 8:
                pack[start:start + 96, :] = left
            else:
                pack[2496:2560, :] = left[0:64]
                pack[2352:2384, :] += jnp.where(lane >= 64, part[64:96], 0.0)
    for a in range(3):
        product = mm_tn(p32[(15 + a) * 32:(19 + a) * 32, :], d2[64:192, :])
        for b in range(3):
            part = fold_taps(product, 32, 16, a, b)
            start = 1728 + (a * 3 + b) * 48
            pack[start:start + 48, :] += jnp.where((lane >= 64) & (lane < 96), part, 0.0)
    fold1 = fold_matrix(256, 16, 96)
    for a in range(3):
        product = mm_tn(v3[(32 + a) * 64:(40 + a) * 64, :], d1[128:640, :])
        for c in range(3):
            high, low = halves(jnp.where(band == c, product, 0.0))
            sums = mm_tn(pick_ref[...], high) + mm_tn(pick_ref[...], low)
            start = 1728 + (a * 3 + c) * 16
            pack[start:start + 16, :] += mm2(sums, fold1)

    def fold_lift(product, fine, chans, matrix):
        kin = iota((fine, 256), 1) >> log2(chans)
        total = jnp.zeros((fine, 256), F32)
        for k in range(256 // chans):
            total = total + jnp.where(kin == k, product[k * fine:(k + 1) * fine], 0.0)
        return mm2(total, matrix)

    pack[2160:2192, :] += fold_lift(gl3, 32, 64, fold_matrix(256, 64, 64))
    pack[2192:2208, :] += fold_lift(gl2, 16, 32, fold2)
    high, low = halves(gh * headmask_ref[...])
    heads = mm_tn(rowrep_ref[...], high) + mm_tn(rowrep_ref[...], low)
    pack[2208:2224, :] += mm2(heads, fold_matrix(256, 16, 64))
    lift4 = fold_lift(gl4, 64, 128, fold4)
    pack[2224:2288, :] += jnp.where(lane >= 64, pltpu.roll(lift4, 64, 1), 0.0)
    pack[2288:2352, :] += jnp.where(lane >= 64, lift4, 0.0)
    share_ref[...] = pack[rows(own_part * SHARE, SHARE, SHARE), :].astype(BF)


def unpack_kernel(full_ref, order_ref, g1_ref, g2_ref, g3_ref, g4_ref, l4_ref, l3_ref, l2_ref, head_ref):
    scale = float(512 * 64 * 16) ** -0.5

    def left(start, count):
        return full_ref[start:start + count, :].astype(F32) * scale

    def right(start, count):
        return pltpu.roll(left(start, count), 64, 1)

    g4_ref[...] = left(0, 1728)
    g3_ref[0:832, :] = left(1728, 832)[:, 0:64]
    g3_ref[832:864, :] = right(2352, 32)[:, 0:64]
    g2_ref[...] = right(1728, 432)[:, 0:32]
    for c in range(3):
        turned = mm_tn(full_ref[1728:1872, :], order_ref[c]) * scale
        g1_ref[c] = turned[96:112, 0:27]
    l3_ref[...] = right(2160, 32)[:, 0:64]
    l2_ref[...] = right(2192, 16)[:, 0:32]
    head_ref[...] = right(2208, 16)[0:3, 0:16]
    l4_ref[:, 0:64] = right(2224, 64)[:, 0:64]
    l4_ref[:, 64:128] = left(2288, 64)[:, 64:128]


def constants():
    lanes = np.arange(128)
    kin = np.where(lanes < 96, (lanes % 48) // 3, -9)
    chan = np.where(lanes < 96, lanes % 3, -9)
    second = (lanes >= 48) & (lanes < 96)
    rowrep = (second[:, None] & (chan[:, None] == np.arange(16)[None, :])).astype(np.float32)
    headmask = (second[:, None] & (kin[:, None] == (np.arange(256) // 16)[None, :])).astype(np.float32)
    place = np.zeros((6, 128, 128), np.float32)
    for part in range(2):
        for c in range(3):
            for row in range(128):
                place[part * 3 + c, row, part * 48 + (row % 16) * 3 + c] = 1.0
    unplace = place.transpose(0, 2, 1)
    pick = np.zeros((256, 16), np.float32)
    band = np.full((256, 256), -9, np.int32)
    base = np.full((256, 128), -99, np.int32)
    order = np.zeros((3, 144, 128), np.float32)
    for b, lead in enumerate((0, 48, 128)):
        for k in range(16):
            for c in range(3):
                pick[lead + k * 3 + c, b * 3 + c] = 1.0
                band[lead + k * 3 + c] = k - np.arange(256) // 16 + 1
                base[lead + k * 3 + c] = lanes - 32 * c - 3 * b
    for tap in range(27):
        a, b, step = tap // 9, tap // 3 % 3, tap % 3
        for c in range(3):
            order[c, (a * 3 + step) * 16 + b * 3 + c, tap] = 1.0
    return order, base, band, pick, rowrep, headmask, place, unplace


def run_build(weights, interpret=False):
    _, base, band, _, rowrep, headmask, _, _ = constants()
    k1, k2, k3, k4, l4, l3, l2, head = weights
    shapes = ((3, 256, 256),) + ((3, 384, 256),) * 3 + ((256, 256),) * 3 + ((128, 256),) * 4
    return pl.pallas_call(
        build_kernel,
        out_shape=tuple(jax.ShapeDtypeStruct(shape, BF) for shape in shapes),
        scratch_shapes=[pltpu.VMEM((128, 256), F32)],
        compiler_params=pltpu.CompilerParams(vmem_limit_bytes=24 * 1024 * 1024),
        interpret=interpret,
    )(
        k1.transpose(2, 1, 0),
        k2.transpose(0, 2, 1).reshape(432, 32),
        k3.transpose(0, 2, 1).reshape(864, 64),
        k4.transpose(0, 2, 1).reshape(1728, 128),
        l4,
        l3,
        l2,
        head,
        jnp.asarray(band),
        jnp.asarray(base),
        jnp.asarray(rowrep, BF),
        jnp.asarray(headmask, F32),
    )


def run_main(where, own, tiles, matrices, interpret=False):
    _, _, band, pick, rowrep, headmask, _, unplace = constants()
    vm = pl.BlockSpec(memory_space=pltpu.VMEM)

    def buf(shape, kind=BF):
        return pltpu.VMEM(shape, kind)

    scratch = [
        buf((512, 128), F32),
        buf((72 * 64, 128)),
        buf((74 * 64, 256)),
        buf((72 * 64, 256), F32),
        buf((72 * 64, 256)),
        buf((36 * 32, 256), F32),
        buf((36 * 32, 256)),
        buf((224, 256), F32),
        buf((224, 256)),
        buf((36 * 32, 384)),
        buf((18 * 16, 384)),
        buf((9 * 8, 384), F32),
        buf((512, 256)),
        buf((36 * 32, 128)),
        buf((160, 128)),
        buf((36 * 32, 256)),
        buf((160, 256)),
        buf((768, 256)),
        buf((256, 256)),
        buf((96, 256)),
        buf((40, 256), F32),
        buf((192, 128), F32),
        buf((256, 128), F32),
        buf((128, 128), F32),
        buf((128, 128), F32),
        buf((512, 128), F32),
        buf((PACK, 128), F32),
    ]
    return pl.pallas_call(
        main_kernel,
        out_shape=(
            jax.ShapeDtypeStruct((3, 8, 128), F32),
            jax.ShapeDtypeStruct((3, 8, 128), F32),
            jax.ShapeDtypeStruct((SHARE, 128), BF),
        ),
        in_specs=[pl.BlockSpec(memory_space=pltpu.SMEM)] + [vm] * 18,
        out_specs=(vm, vm, vm),
        scratch_shapes=scratch,
        compiler_params=pltpu.CompilerParams(vmem_limit_bytes=44 * 1024 * 1024),
        interpret=interpret,
    )(
        where,
        own,
        tiles,
        *matrices,
        jnp.asarray(band),
        jnp.asarray(pick, BF),
        jnp.asarray(rowrep, BF),
        jnp.asarray(headmask, F32),
        jnp.asarray(unplace, BF),
    )


def run_prep(velocity, cotangent, interpret=False):
    place = constants()[6]
    return pl.pallas_call(
        prep_kernel,
        out_shape=jax.ShapeDtypeStruct((48, 128), BF),
        interpret=interpret,
    )(velocity, cotangent, jnp.asarray(place, BF))


def unpack(full, interpret=False):
    order = constants()[0]
    shapes = ((3, 16, 27), (432, 32), (864, 64), (1728, 128), (64, 128), (32, 64), (16, 32), (3, 16))
    g1, g2, g3, g4, l4, l3, l2, head = pl.pallas_call(
        unpack_kernel,
        out_shape=tuple(jax.ShapeDtypeStruct(shape, F32) for shape in shapes),
        interpret=interpret,
    )(full, jnp.asarray(order, BF))
    return (
        g1.transpose(2, 1, 0),
        g2.reshape(27, 16, 32).transpose(0, 2, 1),
        g3.reshape(27, 32, 64).transpose(0, 2, 1),
        g4.reshape(27, 64, 128).transpose(0, 2, 1),
        l4,
        l3,
        l2,
        head,
    )


FAR = (4, -1, -4, 1, 3, -2, -3, 2)
GROUP_Y = [[8 * z + y for y in range(8)] for z in range(8)]
GROUP_Z = [[8 * z + y for z in range(8)] for y in range(8)]


def exchange(x, groups):
    return lax.all_to_all(x, "wide", 0, 0, axis_index_groups=groups, tiled=True)


def local(velocity, cotangent, *weights):
    where = jnp.stack([lax.axis_index("narrow")] + [4 + step for step in FAR]).astype(jnp.int32)
    tile = run_prep(velocity, cotangent)
    own = lax.all_gather(tile, "narrow", axis=0)
    routes = [((w + FAR[n]) % 64 * 8 + n, w * 8 + n) for w in range(64) for n in range(8)]
    far = lax.ppermute(own, ("wide", "narrow"), routes)
    tiles = lax.all_gather(far, "narrow", axis=0)
    prediction, grad_velocity, share = run_main(where, own, tiles, run_build(weights))
    pieces = exchange(share.reshape(8, PIECE, 128), GROUP_Y)
    partial = pieces.astype(F32).sum(axis=0).astype(BF)
    pieces = exchange(jnp.broadcast_to(partial, (8, PIECE, 128)), GROUP_Z)
    total = pieces.astype(F32).sum(axis=0).astype(BF)
    whole = exchange(jnp.broadcast_to(total, (8, PIECE, 128)), GROUP_Y).reshape(SHARE, 128)
    full = lax.all_gather(whole, "narrow", axis=0).reshape(PACK, 128)
    return (prediction, grad_velocity) + unpack(full)


def solution(mesh):
    split = P(None, "wide", "narrow")
    return jax.shard_map(
        local,
        mesh=mesh,
        in_specs=(split, split) + (P(),) * 8,
        out_specs=(split, split) + (P(),) * 8,
        check_vma=False,
    )
```

time: 1130 us -> 126 us (0.11)
  local copies, waits for them, and re-layouts: 451 us -> 5.45 us
  waiting for transfers between devices: 419 us -> 1.89 us
  starting transfers between devices: 92.9 us -> 2.04 us
  matrix products: 30.4 us -> 0 us
  Pallas kernels: 0 us -> 25.7 us
  other arithmetic: 16.9 us -> 0.03 us
  between operations: 14.9 us -> 0.76 us
  blocking collectives: 102 us -> 90 us
    gather x31 -> x0, local copies, waits for them, and re-layouts: 441 us -> none  [the longest x12 422 us: unfold(): picked = jnp.take(extended, jnp.asarray(table), axis=1)]
    psum x2 -> x0, waiting for transfers between devices: 413 us -> none  [local(): lax.psum((grad_head, grad_lift_two, grad_lift_three, grad_lift_four, grad...]
    ppermute x20 -> x1, starting transfers between devices: 92.6 us -> 2.04 us  [local(): far = lax.ppermute(own, ('wide', 'narrow'), routes)]
    all_gather x4 -> x3, blocking collectives: 102 us -> 59.2 us  [the longest x1 21 us: local(): tiles = lax.all_gather(far, 'narrow', axis=0)]
    all_to_all x0 -> x3, blocking collectives: none -> 30.8 us  [exchange(): return lax.all_to_all(x, 'wide', 0, 0, axis_index_groups=groups, tiled=True)]
    dot_general x24 -> x0, matrix products: 30.4 us -> none  [the longest x8 17.2 us: correlate(): return jnp.dot(matrix, columns, preferred_element_type=jnp.float32)]
    pallas_call x0 -> x4, Pallas kernels: none -> 25.7 us  [the longest x1 19.8 us: run_main(): pl.pallas_call(main_kernel, out_shape=(jax.ShapeDtypeStruct((3, 8, 128),...]
  transfers between devices with their start and end apart: 22 -> 1, of which waited for: 7 -> 1; matrix products, arithmetic and copies ran while one was open for 12% -> 0% of each run, Pallas kernels for 0% -> 1%
where the time goes in v1:
time: 126 us
  blocking collectives  90 us (71%)
  Pallas kernels  25.7 us (20%)
  local copies, waits for them, and re-layouts  5.45 us (4%)
  starting transfers between devices  2.04 us (2%)
  waiting for transfers between devices  1.89 us (2%)
    all_to_all x3, blocking collectives, exchange(): return lax.all_to_all(x, 'wide', 0, 0, axis_index_groups=groups, tiled=True)  30.8 us
    all_gather x1, blocking collectives, local(): tiles = lax.all_gather(far, 'narrow', axis=0)  21 us
    pallas_call x1, Pallas kernels, run_main(): pl.pallas_call(main_kernel, out_shape=(jax.ShapeDtypeStruct((3, 8, 128),...  19.8 us
    all_gather x1, blocking collectives, local(): own = lax.all_gather(tile, 'narrow', axis=0)  19.8 us
    all_gather x1, blocking collectives, local(): full = lax.all_gather(whole, 'narrow', axis=0).reshape(PACK, 128)  18.4 us
    unnamed x30, local copies, waits for them, and re-layouts  5.33 us
  transfers between devices with their start and end apart: 1, of which 1 were waited for; matrix products, arithmetic and copies ran while one was open for 0% of the time, Pallas kernels for 1%

profile of v1, /device:TPU:1, one launch (start us, length us, event | category | flops | bytes accessed | tf_op | source)
XLA Modules:
  0.0 125.9 jit_solution(13803596888591573005)
XLA Ops:
  0.6 0.0 copy-start
  0.7 2.1 %shard_map.276 = bf16[48,128]{1,0:T(8,128)(2,1)} custom-call(bf16[3,8,128]{2,1,0:T(8,128)(2,1)} %vel_ref.1, bf16[3,8,128]{2,1,0:T(8,128)(2,1)} %cot_ref.1, bf16[6,128,128]{2,1,0:T(8,128)(2,1)} %constant.40.clone.place_ref), custom_call_target="tpu_custom_call" | custom-call | tf_op jit(solution)/shard_map/pallas_call | solution.py:648
  2.8 19.8 %all-gather = bf16[384,128]{1,0:T(8,128)(2,1)S(1)} all-gather(bf16[48,128]{1,0:T(8,128)(2,1)} %shard_map.276), channel_id=2, replica_groups=mesh['wide'=64,'narrow'=8] {'narrow'}, dimensions={0}, use_global_device_ids=true | all-gather | bytes 110592 | tf_op jit(solution)/shard_map/all_gather | solution.py:687
  22.5 2.0 %collective-permute-start = (bf16[8,48,128]{2,1,0:T(8,128)(2,1)S(1)}, bf16[8,48,128]{2,1,0:T(8,128)(2,1)S(1)}, u32[]{:S(2)}, u32[]{:S(2)}) collective-permute-start(bf16[8,48,128]{2,1,0:T(8,128)(2,1)S(1)} %bitcast.28), channel_id=1, source_target_pairs={{32,0},{505,1},{482,2},{11,3},{28,4},{501,5},{494,6},{23,7},{40,8}... | collective-permute-start | bytes 294920 | tf_op jit(solution)/shard_map/ppermute | solution.py:689
  24.6 0.1 stack.7.where_ref
  24.7 0.6 copy-done.13
  25.4 0.0 copy-done.14
  25.4 0.9 copy-done.1
  26.3 1.0 copy-done.3
  27.3 0.9 copy-done.4
  28.2 0.9 copy-done.7
  29.1 0.9 copy-done.8
  30.0 1.2 shard_map.277
  31.3 0.0 copy-start.2
  31.3 0.0 copy-start.5
  31.3 1.9 %collective-permute-done = bf16[8,48,128]{2,1,0:T(8,128)(2,1)S(1)} collective-permute-done((bf16[8,48,128]{2,1,0:T(8,128)(2,1)S(1)}, bf16[8,48,128]{2,1,0:T(8,128)(2,1)S(1)}, u32[]{:S(2)}, u32[]{:S(2)}) %collective-permute-start) | collective-permute-done | bytes 98336 | tf_op jit(solution)/shard_map/ppermute | solution.py:689
  33.2 21.0 %all-gather.1 = bf16[64,48,128]{2,1,0:T(8,128)(2,1)S(1)} all-gather(bf16[8,48,128]{2,1,0:T(8,128)(2,1)S(1)} %collective-permute-done), channel_id=3, replica_groups=mesh['wide'=64,'narrow'=8] {'narrow'}, dimensions={0}, use_global_device_ids=true | all-gather | bytes 884736 | tf_op jit(solution)/shard_map/all_gather | solution.py:690
  54.2 0.0 copy-done.5
  54.2 19.8 %shard_map.278 = (f32[3,8,128]{2,1,0:T(8,128)}, f32[3,8,128]{2,1,0:T(8,128)}, bf16[320,128]{1,0:T(8,128)(2,1)S(1)}) custom-call(s32[9]{0:T(128)S(1)} %stack.7.where_ref, bf16[8,48,128]{2,1,0:T(8,128)(2,1)S(1)} %bitcast.29, bf16[8,8,48,128]{3,2,1,0:T(8,128)(2,1)S(1)} %bitcast.26, bf16[3,256,256]{2,1,0:T(8,128)(2,1)S(1)} %get-tuple-element.32.t1, ...), custom_call_target="tpu_custom_call" | custom-call | tf_op jit(solution)/shard_map/pallas_call | solution.py:621
  74.1 9.9 %all_to_all.15 = bf16[8,40,128]{2,1,0:T(8,128)(2,1)S(1)} all-to-all(bf16[8,40,128]{2,1,0:T(8,128)(2,1)S(1)} %bitcast.32), channel_id=1, replica_groups={{0,8,16,24,32,40,48,56},{64,72,80,88,96,104,112,120},{128,136,144,152,1..., dimensions={0} | all-to-all | bytes 163840 | tf_op jit(solution)/shard_map/all_to_all | solution.py:681
  84.0 11.1 %all_to_all.16 = bf16[8,40,128]{2,1,0:T(8,128)(2,1)S(1)} all-to-all(bf16[8,40,128]{2,1,0:T(8,128)(2,1)S(1)} %broadcast_in_dim.6), channel_id=1, replica_groups={{0,64,128,192,256,320,384,448},{8,72,136,200,264,328,392,456},{16,80,14..., dimensions={0} | all-to-all | bytes 163840 | tf_op jit(solution)/shard_map/all_to_all | solution.py:681
  95.2 9.8 %all_to_all.17 = bf16[8,40,128]{2,1,0:T(8,128)(2,1)S(1)} all-to-all(bf16[8,40,128]{2,1,0:T(8,128)(2,1)S(1)} %broadcast_in_dim.7), channel_id=1, replica_groups={{0,8,16,24,32,40,48,56},{64,72,80,88,96,104,112,120},{128,136,144,152,1..., dimensions={0} | all-to-all | bytes 163840 | tf_op jit(solution)/shard_map/all_to_all | solution.py:681
  105.0 18.4 %all_gather.19 = bf16[8,320,128]{2,1,0:T(8,128)(2,1)} all-gather(bf16[1,320,128]{2,1,0:T(8,128)(2,1)S(1)} %bitcast.35), channel_id=1, replica_groups=mesh['wide'=64,'narrow'=8] {'narrow'}, dimensions={0}, use_global_device_ids=true | all-gather | bytes 737280 | tf_op jit(solution)/shard_map/all_gather | solution.py:697
  123.4 2.5 %shard_map.279 = (f32[3,16,27]{2,1,0:T(8,128)}, f32[432,32]{1,0:T(8,128)}, f32[864,64]{1,0:T(8,128)}, f32[1728,128]{1,0:T(8,128)}, f32[64,128]{1,0:T(8,128)}, /*...) custom-call(bf16[2560,128]{1,0:T(8,128)(2,1)} %bitcast.34, bf16[3,144,128]{2,1,0:T(8,128)(2,1)} %constant.47.clone.order_ref), custom_call_target="tpu_custom_call" | custom-call | tf_op jit(solution)/shard_map/pallas_call | solution.py:658
  (23 shorter events, 0.1 us)
Async XLA Ops:
  0.6 24.0 %copy-start = (s32[256,256]{1,0:T(8,128)S(1)}, s32[256,256]{1,0:T(8,128)}, u32[]{:S(2)}) copy-start(s32[256,256]{1,0:T(8,128)} %constant.41.clone.band_ref) | copy-start | bytes 786436
  2.8 21.9 %copy-start.6 = (bf16[128,16]{1,0:T(8,128)(2,1)S(1)}, bf16[128,16]{1,0:T(8,128)(2,1)}, u32[]{:S(2)}) copy-start(bf16[128,16]{1,0:T(8,128)(2,1)} %constant.43.clone.rowrep_ref) | copy-start | bytes 12292
  2.8 21.9 %copy-start.11 = (bf16[27,16,3]{0,1,2:T(8,128)(2,1)S(1)}, bf16[27,16,3]{0,1,2:T(8,128)(2,1)}, u32[]{:S(2)}) copy-start(bf16[27,16,3]{0,1,2:T(8,128)(2,1)} %param.23) | copy-start | bytes 7780
  2.8 21.9 %copy-start.12 = (bf16[32,64]{1,0:T(8,128)(2,1)S(1)}, bf16[32,64]{1,0:T(8,128)(2,1)}, u32[]{:S(2)}) copy-start(bf16[32,64]{1,0:T(8,128)(2,1)} %l3_ref.1) | copy-start | bytes 12292
  22.5 2.2 %copy-start.10 = (bf16[64,128]{1,0:T(8,128)(2,1)S(1)}, bf16[64,128]{1,0:T(8,128)(2,1)}, u32[]{:S(2)}) copy-start(bf16[64,128]{1,0:T(8,128)(2,1)} %l4_ref.1) | copy-start | bytes 49156
  22.5 10.7 %collective-permute-start = (bf16[8,48,128]{2,1,0:T(8,128)(2,1)S(1)}, bf16[8,48,128]{2,1,0:T(8,128)(2,1)S(1)}, u32[]{:S(2)}, u32[]{:S(2)}) collective-permute-start(bf16[8,48,128]{2,1,0:T(8,128)(2,1)S(1)} %bitcast.28), channel_id=1, source_target_pairs={{32,0},{505,1},{482,2},{11,3},{28,4},{501,5},{494,6},{23,7},{40,8}... | collective-permute-start | bytes 294920 | tf_op jit(solution)/shard_map/ppermute | solution.py:689
  24.7 0.7 copy-start.13
  24.7 0.7 copy-start.14
  25.4 0.9 copy-start.1
  26.3 1.0 copy-start.3
  27.3 0.9 copy-start.4
  28.2 0.9 copy-start.7
  29.1 0.9 copy-start.8
  31.3 22.9 %copy-start.2 = (f32[128,256]{1,0:T(8,128)S(1)}, f32[128,256]{1,0:T(8,128)}, u32[]{:S(2)}) copy-start(f32[128,256]{1,0:T(8,128)} %constant.44.clone.headmask_ref) | copy-start | bytes 393220
  31.3 22.9 %copy-start.5 = (bf16[6,128,128]{2,1,0:T(8,128)(2,1)S(1)}, bf16[6,128,128]{2,1,0:T(8,128)(2,1)}, u32[]{:S(2)}) copy-start(bf16[6,128,128]{2,1,0:T(8,128)(2,1)} %constant.46.clone.unplace_ref) | copy-start | bytes 589828
  33.2 21.0 %copy-start.9 = (bf16[256,16]{1,0:T(8,128)(2,1)S(1)}, bf16[256,16]{1,0:T(8,128)(2,1)}, u32[]{:S(2)}) copy-start(bf16[256,16]{1,0:T(8,128)(2,1)} %constant.45.clone.pick_ref) | copy-start | bytes 24580

commit v2 on v1

--- a/solution.py
+++ b/solution.py
@@ -63,6 +63,31 @@
 def fold_matrix(rows, chans, lead):
     row, col = iota((rows, 128), 0), iota((rows, 128), 1)
     return one_hot((row & (chans - 1)) + lead == col)
+
+
+def packed(shape):
+    row = iota(shape, 0)
+    b = jnp.where(row < 48, 0, jnp.where(row < 96, 1, 2))
+    left = row - jnp.where(row < 48, 0, jnp.where(row < 96, 48, 128))
+    kin = (left * 43) >> 7
+    valid = (row < 96) | ((row >= 128) & (row < 176))
+    return valid, b, kin, left - 3 * kin
+
+
+def band_matrix():
+    valid, _, kin, _ = packed((256, 256))
+    return jnp.where(valid, kin - (iota((256, 256), 1) >> 4) + 1, -9)
+
+
+def head_matrices():
+    row = iota((128, 16), 0)
+    _, _, _, chan = packed((128, 16))
+    second = (row >= 48) & (row < 96)
+    rowrep = one_hot(second & (chan == iota((128, 16), 1)))
+    row = iota((128, 256), 0)
+    _, _, kin, _ = packed((128, 256))
+    second = (row >= 48) & (row < 96)
+    return rowrep, second & (kin == (iota((128, 256), 1) >> 4))
 
 
 def shift_y(v, count, step):
@@ -89,7 +114,7 @@
     return (0.5 + 0.5 * bend) * (1.0 + half * (1.0 - bend))
 
 
-def prep_kernel(vel_ref, cot_ref, place_ref, out_ref):
+def prep_kernel(vel_ref, cot_ref, out_ref):
     row, col = iota((64, 128), 0), iota((64, 128), 1)
     mask = (row & 7) == (col >> 4)
     spread = one_hot((iota((64, 8), 0) >> 3) == iota((64, 8), 1))
@@ -98,29 +123,28 @@
         for chan in range(3):
             wide = mm(spread, ref[chan])
             kept = jnp.where(mask, wide, 0.0).astype(BF)
-            total = total + mm(kept, place_ref[part * 3 + chan])
+            place = one_hot(
+                iota((128, 128), 1) - (part * 48 + chan) == 3 * (iota((128, 128), 0) & 15)
+            )
+            total = total + mm(kept, place)
     last = total[48:64]
     spare = iota((16, 128), 1) >= 96
     for g in range(3):
         moved = pltpu.roll(last, 96 - 32 * g, 1)
-        out_ref[g * 16:(g + 1) * 16, :] = jnp.where(
-            spare, moved, total[g * 16:(g + 1) * 16]
-        ).astype(BF)
+        rows = jnp.where(spare, moved, total[g * 16:(g + 1) * 16]).astype(BF)
+        for copy in range(8):
+            out_ref[copy, g * 16:(g + 1) * 16, :] = rows
 
 
 def build_kernel(
-    k1_ref,
-    k2_ref,
-    k3_ref,
-    k4_ref,
-    l4_ref,
-    l3_ref,
-    l2_ref,
-    head_ref,
-    band_ref,
-    base_ref,
-    rowrep_ref,
-    headmask_ref,
+    k1_far,
+    k2_far,
+    k3_far,
+    k4_far,
+    l4_far,
+    l3_far,
+    l2_far,
+    head_far,
     t1,
     t2,
     t3,
@@ -133,7 +157,31 @@
     b3,
     b2,
     small,
+    k1_ref,
+    k2_ref,
+    k3_ref,
+    k4_ref,
+    l4_ref,
+    l3_ref,
+    l2_ref,
+    head_ref,
+    sems,
 ):
+    far = (k2_far, k3_far, k4_far, k1_far, l4_far, l3_far, l2_far, head_far)
+    near = (k2_ref, k3_ref, k4_ref, k1_ref, l4_ref, l3_ref, l2_ref, head_ref)
+    copies = [
+        pltpu.make_async_copy(source, target, sems.at[i])
+        for i, (source, target) in enumerate(zip(far, near))
+    ]
+    for copy in copies:
+        copy.start()
+    band = band_matrix()
+    valid, b_row, _, chan = packed((256, 128))
+    base = jnp.where(valid, iota((256, 128), 1) - 32 * chan - 3 * b_row, -99)
+    rowrep, headmask = head_matrices()
+    for copy in copies:
+        copy.wait()
+
     def build(kernel_ref, t_ref, outs, ins):
         planes = 128 // ins
         rep = mm(kernel_ref[...], tile_matrix(outs, 256))
@@ -156,8 +204,6 @@
     for c in range(3):
         small[c * 32:c * 32 + 27, :] = mm_tn(k1_ref[c], tile_matrix(16, 256))
     rep1 = small[...].astype(BF)
-    base = base_ref[...]
-    band = band_ref[...]
     for a in range(3):
         block = jnp.zeros((256, 256), F32)
         for c in range(3):
@@ -180,29 +226,24 @@
     small[0:3, 0:16] = head_ref[...].astype(F32)
     tileh = one_hot(iota((128, 256), 0) == (iota((128, 256), 1) & 15))
     reph = mm(small[0:16, 0:128].astype(BF), tileh).astype(BF)
-    hp[...] = (mm(rowrep_ref[...], reph) * headmask_ref[...]).astype(BF)
+    hp[...] = jnp.where(headmask, mm(rowrep, reph), 0.0).astype(BF)
 
 
 def main_kernel(
     where_ref,
-    own_ref,
-    tiles_ref,
-    t1,
-    t2,
-    t3,
-    t4,
-    f4,
-    f3,
-    f2,
-    hp,
-    b4,
-    b3,
-    b2,
-    band_ref,
-    pick_ref,
-    rowrep_ref,
-    headmask_ref,
-    unplace_ref,
+    own_far,
+    tiles_far,
+    t1_far,
+    t2_far,
+    t3_far,
+    t4_far,
+    f4_far,
+    f3_far,
+    f2_far,
+    hp_far,
+    b4_far,
+    b3_far,
+    b2_far,
     pred_ref,
     gradv_ref,
     share_ref,
@@ -233,10 +274,43 @@
     ups_b,
     line,
     pack,
+    own_ref,
+    tiles_ref,
+    t1,
+    t2,
+    t3,
+    t4,
+    f4,
+    f3,
+    f2,
+    hp,
+    b4,
+    b3,
+    b2,
+    sems,
 ):
+    far = (t1_far, t2_far, t3_far, t4_far, f4_far, f3_far, f2_far, hp_far, b4_far, b3_far, b2_far)
+    near = (t1, t2, t3, t4, f4, f3, f2, hp, b4, b3, b2)
+    copies = [
+        pltpu.make_async_copy(source, target, sems.at[9 + i])
+        for i, (source, target) in enumerate(zip(far, near))
+    ]
+    own_copy = pltpu.make_async_copy(own_far, own_ref, sems.at[8])
+    own_copy.start()
+
+    def line_copy(step):
+        return pltpu.make_async_copy(tiles_far.at[step], tiles_ref.at[step], sems.at[step])
+
+    for step in range(8):
+        line_copy(step).start()
+    for copy in copies:
+        copy.start()
     own_part = where_ref[0]
     lane = iota((1, 128), 1)
-    band = band_ref[...]
+    band = band_matrix()
+    valid, b_row, _, chan_row = packed((256, 16))
+    pick = one_hot(valid & (iota((256, 16), 1) == 3 * b_row + chan_row))
+    rowrep, headmask = head_matrices()
 
     pool1, pool2, pool3 = pool_matrix(16), pool_matrix(32), pool_matrix(64)
 
@@ -267,11 +341,15 @@
             v3[spot, 128:256] = high.astype(BF)
 
     def arrange_far(step, _):
+        line_copy(step).wait()
         arrange(lambda n: tiles_ref[step, n], where_ref[1 + step])
         return 0
 
+    own_copy.wait()
     arrange(lambda n: own_ref[n], 4)
     lax.fori_loop(0, 8, arrange_far, 0)
+    for copy in copies:
+        copy.wait()
 
     def pooled(field, matrix, count):
         flat = mm(field, matrix)
@@ -429,7 +507,9 @@
     mask = (iota((64, 128), 0) & 7) == (iota((64, 128), 1) >> 4)
     for part, ref in ((0, gradv_ref), (1, pred_ref)):
         for chan in range(3):
-            matrix = unplace_ref[part * 3 + chan]
+            matrix = one_hot(
+                iota((128, 128), 0) - (part * 48 + chan) == 3 * (iota((128, 128), 1) & 15)
+            )
             full = mm(first, matrix) + mm(second, matrix) + mm(third, matrix)
             full = jnp.where(mask, full, 0.0).reshape(8, 8, 128)
             ref[chan] = jnp.sum(full, axis=1)
@@ -481,7 +561,7 @@
         product = mm_tn(v3[(32 + a) * 64:(40 + a) * 64, :], d1[128:640, :])
         for c in range(3):
             high, low = halves(jnp.where(band == c, product, 0.0))
-            sums = mm_tn(pick_ref[...], high) + mm_tn(pick_ref[...], low)
+            sums = mm_tn(pick, high) + mm_tn(pick, low)
             start = 1728 + (a * 3 + c) * 16
             pack[start:start + 16, :] += mm2(sums, fold1)
 
@@ -494,8 +574,8 @@
 
     pack[2160:2192, :] += fold_lift(gl3, 32, 64, fold_matrix(256, 64, 64))
     pack[2192:2208, :] += fold_lift(gl2, 16, 32, fold2)
-    high, low = halves(gh * headmask_ref[...])
-    heads = mm_tn(rowrep_ref[...], high) + mm_tn(rowrep_ref[...], low)
+    high, low = halves(jnp.where(headmask, gh, 0.0))
+    heads = mm_tn(rowrep, high) + mm_tn(rowrep, low)
     pack[2208:2224, :] += mm2(heads, fold_matrix(256, 16, 64))
     lift4 = fold_lift(gl4, 64, 128, fold4)
     pack[2224:2288, :] += jnp.where(lane >= 64, pltpu.roll(lift4, 64, 1), 0.0)
@@ -526,45 +606,35 @@
     l4_ref[:, 64:128] = left(2288, 64)[:, 64:128]
 
 
-def constants():
-    lanes = np.arange(128)
-    kin = np.where(lanes < 96, (lanes % 48) // 3, -9)
-    chan = np.where(lanes < 96, lanes % 3, -9)
-    second = (lanes >= 48) & (lanes < 96)
-    rowrep = (second[:, None] & (chan[:, None] == np.arange(16)[None, :])).astype(np.float32)
-    headmask = (second[:, None] & (kin[:, None] == (np.arange(256) // 16)[None, :])).astype(np.float32)
-    place = np.zeros((6, 128, 128), np.float32)
-    for part in range(2):
-        for c in range(3):
-            for row in range(128):
-                place[part * 3 + c, row, part * 48 + (row % 16) * 3 + c] = 1.0
-    unplace = place.transpose(0, 2, 1)
-    pick = np.zeros((256, 16), np.float32)
-    band = np.full((256, 256), -9, np.int32)
-    base = np.full((256, 128), -99, np.int32)
+def order_matrix():
     order = np.zeros((3, 144, 128), np.float32)
-    for b, lead in enumerate((0, 48, 128)):
-        for k in range(16):
-            for c in range(3):
-                pick[lead + k * 3 + c, b * 3 + c] = 1.0
-                band[lead + k * 3 + c] = k - np.arange(256) // 16 + 1
-                base[lead + k * 3 + c] = lanes - 32 * c - 3 * b
     for tap in range(27):
         a, b, step = tap // 9, tap // 3 % 3, tap % 3
         for c in range(3):
             order[c, (a * 3 + step) * 16 + b * 3 + c, tap] = 1.0
-    return order, base, band, pick, rowrep, headmask, place, unplace
+    return order
 
 
 def run_build(weights, interpret=False):
-    _, base, band, _, rowrep, headmask, _, _ = constants()
     k1, k2, k3, k4, l4, l3, l2, head = weights
     shapes = ((3, 256, 256),) + ((3, 384, 256),) * 3 + ((256, 256),) * 3 + ((128, 256),) * 4
     return pl.pallas_call(
         build_kernel,
         out_shape=tuple(jax.ShapeDtypeStruct(shape, BF) for shape in shapes),
-        scratch_shapes=[pltpu.VMEM((128, 256), F32)],
-        compiler_params=pltpu.CompilerParams(vmem_limit_bytes=24 * 1024 * 1024),
+        in_specs=[pl.BlockSpec(memory_space=pltpu.HBM)] * 8,
+        scratch_shapes=[
+            pltpu.VMEM((128, 256), F32),
+            pltpu.VMEM((3, 16, 27), BF),
+            pltpu.VMEM((432, 32), BF),
+            pltpu.VMEM((864, 64), BF),
+            pltpu.VMEM((1728, 128), BF),
+            pltpu.VMEM((64, 128), BF),
+            pltpu.VMEM((32, 64), BF),
+            pltpu.VMEM((16, 32), BF),
+            pltpu.VMEM((3, 16), BF),
+            pltpu.SemaphoreType.DMA((8,)),
+        ],
+        compiler_params=pltpu.CompilerParams(vmem_limit_bytes=60 * 1024 * 1024),
         interpret=interpret,
     )(
         k1.transpose(2, 1, 0),
@@ -575,15 +645,10 @@
         l3,
         l2,
         head,
-        jnp.asarray(band),
-        jnp.asarray(base),
-        jnp.asarray(rowrep, BF),
-        jnp.asarray(headmask, F32),
     )
 
 
 def run_main(where, own, tiles, matrices, interpret=False):
-    _, _, band, pick, rowrep, headmask, _, unplace = constants()
     vm = pl.BlockSpec(memory_space=pltpu.VMEM)
 
     def buf(shape, kind=BF):
@@ -617,6 +682,20 @@
         buf((128, 128), F32),
         buf((512, 128), F32),
         buf((PACK, 128), F32),
+        buf((8, 48, 128)),
+        buf((8, 8, 48, 128)),
+        buf((3, 256, 256)),
+        buf((3, 384, 256)),
+        buf((3, 384, 256)),
+        buf((3, 384, 256)),
+        buf((256, 256)),
+        buf((256, 256)),
+        buf((256, 256)),
+        buf((128, 256)),
+        buf((128, 256)),
+        buf((128, 256)),
+        buf((128, 256)),
+        pltpu.SemaphoreType.DMA((20,)),
     ]
     return pl.pallas_call(
         main_kernel,
@@ -625,35 +704,30 @@
             jax.ShapeDtypeStruct((3, 8, 128), F32),
             jax.ShapeDtypeStruct((SHARE, 128), BF),
         ),
-        in_specs=[pl.BlockSpec(memory_space=pltpu.SMEM)] + [vm] * 18,
+        in_specs=[pl.BlockSpec(memory_space=pltpu.SMEM)]
+        + [pl.BlockSpec(memory_space=pltpu.HBM)] * 13,
         out_specs=(vm, vm, vm),
         scratch_shapes=scratch,
-        compiler_params=pltpu.CompilerParams(vmem_limit_bytes=44 * 1024 * 1024),
+        compiler_params=pltpu.CompilerParams(vmem_limit_bytes=60 * 1024 * 1024),
         interpret=interpret,
     )(
         where,
         own,
         tiles,
         *matrices,
-        jnp.asarray(band),
-        jnp.asarray(pick, BF),
-        jnp.asarray(rowrep, BF),
-        jnp.asarray(headmask, F32),
-        jnp.asarray(unplace, BF),
     )
 
 
 def run_prep(velocity, cotangent, interpret=False):
-    place = constants()[6]
     return pl.pallas_call(
         prep_kernel,
-        out_shape=jax.ShapeDtypeStruct((48, 128), BF),
+        out_shape=jax.ShapeDtypeStruct((8, 48, 128), BF),
         interpret=interpret,
-    )(velocity, cotangent, jnp.asarray(place, BF))
+    )(velocity, cotangent)
 
 
 def unpack(full, interpret=False):
-    order = constants()[0]
+    order = order_matrix()
     shapes = ((3, 16, 27), (432, 32), (864, 64), (1728, 128), (64, 128), (32, 64), (16, 32), (3, 16))
     g1, g2, g3, g4, l4, l3, l2, head = pl.pallas_call(
         unpack_kernel,
@@ -683,8 +757,8 @@
 
 def local(velocity, cotangent, *weights):
     where = jnp.stack([lax.axis_index("narrow")] + [4 + step for step in FAR]).astype(jnp.int32)
-    tile = run_prep(velocity, cotangent)
-    own = lax.all_gather(tile, "narrow", axis=0)
+    copies = run_prep(velocity, cotangent)
+    own = lax.all_to_all(copies, "narrow", 0, 0, tiled=True)
     routes = [((w + FAR[n]) % 64 * 8 + n, w * 8 + n) for w in range(64) for n in range(8)]
     far = lax.ppermute(own, ("wide", "narrow"), routes)
     tiles = lax.all_gather(far, "narrow", axis=0)

time: 126 us -> 125 us (level)
  local copies, waits for them, and re-layouts: 5.45 us -> 0.64 us
  waiting for transfers between devices: 1.89 us -> 5.34 us
  Pallas kernels: 25.7 us -> 28.7 us
  blocking collectives: 90 us -> 87.1 us
    all_gather x1 -> x0, blocking collectives: 19.8 us -> none  [local(): own = lax.all_gather(tile, 'narrow', axis=0)]
    all_to_all x0 -> x1, blocking collectives: none -> 15.1 us  [local(): own = lax.all_to_all(copies, 'narrow', 0, 0, tiled=True)]
    unnamed x30 -> x2, local copies, waits for them, and re-layouts: 5.33 us -> 0.01 us
    ppermute x1, waiting for transfers between devices: 1.89 us -> 5.34 us  [local(): far = lax.ppermute(own, ('wide', 'narrow'), routes)]
    all_to_all x3, blocking collectives: 30.8 us -> 33.9 us  [exchange(): return lax.all_to_all(x, 'wide', 0, 0, axis_index_groups=groups, tiled=True)]
    pallas_call x1, Pallas kernels: 1.25 us -> 3.34 us  [run_build(): pl.pallas_call(build_kernel, out_shape=tuple((jax.ShapeDtypeStruct(shape,...]
    all_gather x1, blocking collectives: 21 us -> 19.7 us  [local(): tiles = lax.all_gather(far, 'narrow', axis=0)]
  transfers between devices with their start and end apart: 1 -> 1, of which waited for: 1 -> 1; matrix products, arithmetic and copies ran while one was open for 0% -> 0% of each run, Pallas kernels for 1% -> 3%
where the time goes in v2:
time: 125 us; the launch traced here: 124 us
  blocking collectives  87.1 us (70%)
  Pallas kernels  28.7 us (23%)
  waiting for transfers between devices  5.34 us (4%)
  starting transfers between devices  1.91 us (2%)
    all_to_all x3, blocking collectives, exchange(): return lax.all_to_all(x, 'wide', 0, 0, axis_index_groups=groups, tiled=True)  33.9 us
    pallas_call x1, Pallas kernels, run_main(): pl.pallas_call(main_kernel, out_shape=(jax.ShapeDtypeStruct((3, 8, 128),...  21 us
    all_gather x1, blocking collectives, local(): tiles = lax.all_gather(far, 'narrow', axis=0)  19.7 us
    all_gather x1, blocking collectives, local(): full = lax.all_gather(whole, 'narrow', axis=0).reshape(PACK, 128)  18.4 us
    all_to_all x1, blocking collectives, local(): own = lax.all_to_all(copies, 'narrow', 0, 0, tiled=True)  15.1 us
    ppermute x1, waiting for transfers between devices, local(): far = lax.ppermute(own, ('wide', 'narrow'), routes)  5.34 us
    pallas_call x1, Pallas kernels, run_build(): pl.pallas_call(build_kernel, out_shape=tuple((jax.ShapeDtypeStruct(shape,...  3.34 us
  transfers between devices with their start and end apart: 1, of which 1 were waited for; matrix products, arithmetic and copies ran while one was open for 0% of the time, Pallas kernels for 3%

profile of v2, /device:TPU:1, one launch (start us, length us, event | category | flops | bytes accessed | tf_op | source)
XLA Modules:
  0.0 124.4 jit_solution(15309267610092223080)
XLA Ops:
  0.6 1.9 %shard_map.186 = bf16[8,48,128]{2,1,0:T(8,128)(2,1)} custom-call(bf16[3,8,128]{2,1,0:T(8,128)(2,1)} %vel_ref.1, bf16[3,8,128]{2,1,0:T(8,128)(2,1)} %cot_ref.1), custom_call_target="tpu_custom_call" | custom-call | tf_op jit(solution)/shard_map/pallas_call | solution.py:722
  2.5 15.1 %all_to_all.20.own_far = bf16[8,48,128]{2,1,0:T(8,128)(2,1)S(1)} all-to-all(bf16[8,48,128]{2,1,0:T(8,128)(2,1)} %shard_map.186), channel_id=1, replica_groups=mesh['wide'=64,'narrow'=8] {'narrow'}, dimensions={0} | all-to-all | bytes 196608 | tf_op jit(solution)/shard_map/all_to_all | solution.py:761
  17.6 0.0 copy-start
  17.6 1.9 %collective-permute-start = (bf16[8,48,128]{2,1,0:T(8,128)(2,1)S(1)}, bf16[8,48,128]{2,1,0:T(8,128)(2,1)S(1)}, u32[]{:S(2)}, u32[]{:S(2)}) collective-permute-start(bf16[8,48,128]{2,1,0:T(8,128)(2,1)S(1)} %all_to_all.20.own_far), channel_id=1, source_target_pairs={{32,0},{505,1},{482,2},{11,3},{28,4},{501,5},{494,6},{23,7},{40,8}... | collective-permute-start | bytes 294920 | tf_op jit(solution)/shard_map/ppermute | solution.py:763
  19.5 3.3 %shard_map.187 = (bf16[3,256,256]{2,1,0:T(8,128)(2,1)}, bf16[3,384,256]{2,1,0:T(8,128)(2,1)}, bf16[3,384,256]{2,1,0:T(8,128)(2,1)}, bf16[3,384,256]{2,1,0:T(8,12...) custom-call(bf16[3,16,27]{2,1,0:T(8,128)(2,1)} %bitcast.32, ...), custom_call_target="tpu_custom_call" | custom-call | tf_op jit(solution)/shard_map/pallas_call | solution.py:621
  22.9 0.0 copy-done
  22.9 0.6 stack.7.where_ref
  23.5 5.3 %collective-permute-done = bf16[8,48,128]{2,1,0:T(8,128)(2,1)S(1)} collective-permute-done((bf16[8,48,128]{2,1,0:T(8,128)(2,1)S(1)}, bf16[8,48,128]{2,1,0:T(8,128)(2,1)S(1)}, u32[]{:S(2)}, u32[]{:S(2)}) %collective-permute-start) | collective-permute-done | bytes 98336 | tf_op jit(solution)/shard_map/ppermute | solution.py:763
  28.8 19.7 %all-gather = bf16[64,48,128]{2,1,0:T(8,128)(2,1)} all-gather(bf16[8,48,128]{2,1,0:T(8,128)(2,1)S(1)} %collective-permute-done), channel_id=2, replica_groups=mesh['wide'=64,'narrow'=8] {'narrow'}, dimensions={0}, use_global_device_ids=true | all-gather | bytes 884736 | tf_op jit(solution)/shard_map/all_gather | solution.py:764
  48.6 21.0 %shard_map.188 = (f32[3,8,128]{2,1,0:T(8,128)}, f32[3,8,128]{2,1,0:T(8,128)}, bf16[320,128]{1,0:T(8,128)(2,1)}) custom-call(s32[9]{0:T(128)} %stack.7.where_ref, bf16[8,48,128]{2,1,0:T(8,128)(2,1)} %copy-done, bf16[8,8,48,128]{3,2,1,0:T(8,128)(2,1)} %bitcast.25, bf16[3,256,256]{2,1,0:T(8,128)(2,1)} %get-tuple-element.32.t1_far, ...), custom_call_target="tpu_custom_call" | custom-call | tf_op jit(solution)/shard_map/pallas_call | solution.py:700
  69.6 10.8 %all_to_all.21 = bf16[8,40,128]{2,1,0:T(8,128)(2,1)S(1)} all-to-all(bf16[8,40,128]{2,1,0:T(8,128)(2,1)} %bitcast.31), channel_id=1, replica_groups={{0,8,16,24,32,40,48,56},{64,72,80,88,96,104,112,120},{128,136,144,152,1..., dimensions={0} | all-to-all | bytes 163840 | tf_op jit(solution)/shard_map/all_to_all | solution.py:755
  80.4 13.3 %all_to_all.22 = bf16[8,40,128]{2,1,0:T(8,128)(2,1)S(1)} all-to-all(bf16[8,40,128]{2,1,0:T(8,128)(2,1)S(1)} %broadcast_in_dim.6), channel_id=1, replica_groups={{0,64,128,192,256,320,384,448},{8,72,136,200,264,328,392,456},{16,80,14..., dimensions={0} | all-to-all | bytes 163840 | tf_op jit(solution)/shard_map/all_to_all | solution.py:755
  93.7 9.8 %all_to_all.23 = bf16[8,40,128]{2,1,0:T(8,128)(2,1)S(1)} all-to-all(bf16[8,40,128]{2,1,0:T(8,128)(2,1)S(1)} %broadcast_in_dim.7), channel_id=1, replica_groups={{0,8,16,24,32,40,48,56},{64,72,80,88,96,104,112,120},{128,136,144,152,1..., dimensions={0} | all-to-all | bytes 163840 | tf_op jit(solution)/shard_map/all_to_all | solution.py:755
  103.5 18.4 %all_gather.11 = bf16[8,320,128]{2,1,0:T(8,128)(2,1)} all-gather(bf16[1,320,128]{2,1,0:T(8,128)(2,1)S(1)} %bitcast.28), channel_id=1, replica_groups=mesh['wide'=64,'narrow'=8] {'narrow'}, dimensions={0}, use_global_device_ids=true | all-gather | bytes 737280 | tf_op jit(solution)/shard_map/all_gather | solution.py:771
  121.9 2.5 %shard_map.189 = (f32[3,16,27]{2,1,0:T(8,128)}, f32[432,32]{1,0:T(8,128)}, f32[864,64]{1,0:T(8,128)}, f32[1728,128]{1,0:T(8,128)}, f32[64,128]{1,0:T(8,128)}, /*...) custom-call(bf16[2560,128]{1,0:T(8,128)(2,1)} %bitcast.26, bf16[3,144,128]{2,1,0:T(8,128)(2,1)} %constant.26.clone.order_ref), custom_call_target="tpu_custom_call" | custom-call | tf_op jit(solution)/shard_map/pallas_call | solution.py:732
  (4 shorter events, 0.1 us)
Async XLA Ops:
  17.6 5.3 %copy-start = (bf16[8,48,128]{2,1,0:T(8,128)(2,1)}, bf16[8,48,128]{2,1,0:T(8,128)(2,1)S(1)}, u32[]{:S(2)}) copy-start(bf16[8,48,128]{2,1,0:T(8,128)(2,1)S(1)} %all_to_all.20.own_far) | copy-start | bytes 294916
  17.6 11.2 %collective-permute-start = (bf16[8,48,128]{2,1,0:T(8,128)(2,1)S(1)}, bf16[8,48,128]{2,1,0:T(8,128)(2,1)S(1)}, u32[]{:S(2)}, u32[]{:S(2)}) collective-permute-start(bf16[8,48,128]{2,1,0:T(8,128)(2,1)S(1)} %all_to_all.20.own_far), channel_id=1, source_target_pairs={{32,0},{505,1},{482,2},{11,3},{28,4},{501,5},{494,6},{23,7},{40,8}... | collective-permute-start | bytes 294920 | tf_op jit(solution)/shard_map/ppermute | solution.py:763

commit v3 on v2

--- a/solution.py
+++ b/solution.py
@@ -1,6 +1,5 @@
 import jax
 import jax.numpy as jnp
-import numpy as np
 from jax import lax
 from jax.experimental import pallas as pl
 from jax.experimental.pallas import tpu as pltpu
@@ -10,9 +9,23 @@
 F32 = jnp.float32
 NZ = 16
 LINES = 9
-PIECE = 40
+PIECE = 80
 SHARE = 8 * PIECE
-PACK = 8 * SHARE
+PACK = 4 * SHARE
+PLACES = {
+    "t1": (0, 256),
+    "t2": (768, 384),
+    "t3": (1920, 384),
+    "t4": (3072, 384),
+    "f4": (4224, 256),
+    "f3": (4480, 256),
+    "f2": (4736, 256),
+    "hp": (4992, 128),
+    "b4": (5120, 128),
+    "b3": (5248, 128),
+    "b2": (5376, 128),
+}
+WEIGHT_ROWS = 5504
 
 
 def mm(a, b):
@@ -30,6 +43,22 @@
 def halves(x):
     high = x.astype(BF)
     return high, (x - high.astype(F32)).astype(BF)
+
+
+def taken(weights, name):
+    start, count = PLACES[name]
+    return weights[start:start + count, :]
+
+
+def joint(parts, weights, name):
+    start, count = PLACES[name]
+    return mm(jnp.concatenate(parts, axis=1), weights[start:start + 3 * count, :])
+
+
+def joint_nt(parts, weights, name):
+    start, count = PLACES[name]
+    matrix = [weights[start + a * count:start + (a + 1) * count, :] for a in range(3)]
+    return mm_nt(jnp.concatenate(parts, axis=1), jnp.concatenate(matrix, axis=1))
 
 
 def mm2(x, e):
@@ -145,17 +174,7 @@
     l3_far,
     l2_far,
     head_far,
-    t1,
-    t2,
-    t3,
-    t4,
-    f4,
-    f3,
-    f2,
-    hp,
-    b4,
-    b3,
-    b2,
+    weights,
     small,
     k1_ref,
     k2_ref,
@@ -182,7 +201,7 @@
     for copy in copies:
         copy.wait()
 
-    def build(kernel_ref, t_ref, outs, ins):
+    def build(kernel_ref, place, outs, ins):
         planes = 128 // ins
         rep = mm(kernel_ref[...], tile_matrix(outs, 256))
         kout = iota((ins, 256), 1) >> log2(outs)
@@ -194,12 +213,12 @@
                 for c in range(3):
                     if 0 <= k - c + 1 < planes:
                         block = jnp.where(kout == k - c + 1, taps[c], block)
-                start = b * 128 + k * ins
-                t_ref[a, start:start + ins, :] = block.astype(BF)
-
-    build(k2_ref, t2, 32, 16)
-    build(k3_ref, t3, 64, 32)
-    build(k4_ref, t4, 128, 64)
+                start = place + a * 384 + b * 128 + k * ins
+                weights[start:start + ins, :] = block.astype(BF)
+
+    build(k2_ref, PLACES["t2"][0], 32, 16)
+    build(k3_ref, PLACES["t3"][0], 64, 32)
+    build(k4_ref, PLACES["t4"][0], 128, 64)
     small[...] = jnp.zeros(small.shape, F32)
     for c in range(3):
         small[c * 32:c * 32 + 27, :] = mm_tn(k1_ref[c], tile_matrix(16, 256))
@@ -208,42 +227,35 @@
         block = jnp.zeros((256, 256), F32)
         for c in range(3):
             block = jnp.where(band == c, mm(one_hot(base == 9 * a + c), rep1), block)
-        t1[a] = block.astype(BF)
-
-    def lift(lift_ref, f_ref, b_ref, coarse):
+        weights[a * 256:(a + 1) * 256, :] = block.astype(BF)
+
+    def lift(lift_ref, up, back, coarse):
         fine, chans = lift_ref.shape
         rep = mm(lift_ref[...], tile_matrix(chans, 256))
         kin = iota((fine, 256), 1) >> log2(chans)
         for k in range(2 * coarse):
-            f_ref[k * fine:(k + 1) * fine, :] = jnp.where(kin == k // 2, rep, 0.0).astype(BF)
+            start = PLACES[up][0] + k * fine
+            weights[start:start + fine, :] = jnp.where(kin == k // 2, rep, 0.0).astype(BF)
         for k in range(coarse):
-            b_ref[k * fine:(k + 1) * fine, :] = jnp.where(kin == k, rep, 0.0).astype(BF)
-
-    lift(l4_ref, f4, b4, 2)
-    lift(l3_ref, f3, b3, 4)
-    lift(l2_ref, f2, b2, 8)
+            start = PLACES[back][0] + k * fine
+            weights[start:start + fine, :] = jnp.where(kin == k, rep, 0.0).astype(BF)
+
+    lift(l4_ref, "f4", "b4", 2)
+    lift(l3_ref, "f3", "b3", 4)
+    lift(l2_ref, "f2", "b2", 8)
     small[0:16, 0:128] = jnp.zeros((16, 128), F32)
     small[0:3, 0:16] = head_ref[...].astype(F32)
     tileh = one_hot(iota((128, 256), 0) == (iota((128, 256), 1) & 15))
     reph = mm(small[0:16, 0:128].astype(BF), tileh).astype(BF)
-    hp[...] = jnp.where(headmask, mm(rowrep, reph), 0.0).astype(BF)
+    weights[4992:5120, :] = jnp.where(headmask, mm(rowrep, reph), 0.0).astype(BF)
 
 
 def main_kernel(
     where_ref,
-    own_far,
-    tiles_far,
-    t1_far,
-    t2_far,
-    t3_far,
-    t4_far,
-    f4_far,
-    f3_far,
-    f2_far,
-    hp_far,
-    b4_far,
-    b3_far,
-    b2_far,
+    own_ref,
+    tiles_ref,
+    twins_ref,
+    weights_far,
     pred_ref,
     gradv_ref,
     share_ref,
@@ -274,37 +286,11 @@
     ups_b,
     line,
     pack,
-    own_ref,
-    tiles_ref,
-    t1,
-    t2,
-    t3,
-    t4,
-    f4,
-    f3,
-    f2,
-    hp,
-    b4,
-    b3,
-    b2,
-    sems,
+    weights,
+    sem,
 ):
-    far = (t1_far, t2_far, t3_far, t4_far, f4_far, f3_far, f2_far, hp_far, b4_far, b3_far, b2_far)
-    near = (t1, t2, t3, t4, f4, f3, f2, hp, b4, b3, b2)
-    copies = [
-        pltpu.make_async_copy(source, target, sems.at[9 + i])
-        for i, (source, target) in enumerate(zip(far, near))
-    ]
-    own_copy = pltpu.make_async_copy(own_far, own_ref, sems.at[8])
-    own_copy.start()
-
-    def line_copy(step):
-        return pltpu.make_async_copy(tiles_far.at[step], tiles_ref.at[step], sems.at[step])
-
-    for step in range(8):
-        line_copy(step).start()
-    for copy in copies:
-        copy.start()
+    weights_copy = pltpu.make_async_copy(weights_far, weights, sem)
+    weights_copy.start()
     own_part = where_ref[0]
     lane = iota((1, 128), 1)
     band = band_matrix()
@@ -340,16 +326,18 @@
             v3[spot, 0:128] = low.astype(BF)
             v3[spot, 128:256] = high.astype(BF)
 
-    def arrange_far(step, _):
-        line_copy(step).wait()
+    def arrange_tiles(step, _):
         arrange(lambda n: tiles_ref[step, n], where_ref[1 + step])
         return 0
 
-    own_copy.wait()
+    def arrange_twins(step, _):
+        arrange(lambda n: twins_ref[step, n], where_ref[5 + step])
+        return 0
+
     arrange(lambda n: own_ref[n], 4)
-    lax.fori_loop(0, 8, arrange_far, 0)
-    for copy in copies:
-        copy.wait()
+    lax.fori_loop(0, 4, arrange_tiles, 0)
+    lax.fori_loop(0, 4, arrange_twins, 0)
+    weights_copy.wait()
 
     def pooled(field, matrix, count):
         flat = mm(field, matrix)
@@ -384,9 +372,7 @@
 
     def fine_forward(step, _):
         start = step * 512
-        pre = mm(v3[rows(start, 512, 64), :], t1[0])
-        for a in (1, 2):
-            pre = pre + mm(v3[rows(start + a * 64, 512, 64), :], t1[a])
+        pre = joint([v3[rows(start + a * 64, 512, 64), :] for a in range(3)], weights, "t1")
         pre1[rows(start, 512, 512), :] = pre
         act = silu_of(pre).astype(BF)
         act1[rows(start, 512, 512), :] = act
@@ -398,9 +384,7 @@
 
     def mid_forward(step, _):
         start = (2 + step * 8) * 32
-        pre = mm(p32[rows(start - 32, 256, 32), :], t2[0])
-        for a in (1, 2):
-            pre = pre + mm(p32[rows(start + (a - 1) * 32, 256, 32), :], t2[a])
+        pre = joint([p32[rows(start + (a - 1) * 32, 256, 32), :] for a in range(3)], weights, "t2")
         pre2[rows(start, 256, 32), :] = pre
         act = silu_of(pre).astype(BF)
         act2[rows(start, 256, 32), :] = act
@@ -410,23 +394,19 @@
 
     lax.fori_loop(0, 4, mid_forward, 0)
 
-    pre = mm(p33[16:240, :], t3[0])
-    for a in (1, 2):
-        pre = pre + mm(p33[(1 + a) * 16:(1 + a) * 16 + 224, :], t3[a])
+    pre = joint([p33[(1 + a) * 16:(1 + a) * 16 + 224, :] for a in range(3)], weights, "t3")
     pre3[...] = pre
     act = silu_of(pre).astype(BF)
     act3[...] = act
     half = (pooled(act, pool3, 16) * 0.125).astype(BF).astype(F32)
     put3(p34, 8, 8, half, 8)
 
-    pre4 = mm(p34[8:48, :].astype(BF), t4[0])
-    for a in (1, 2):
-        pre4 = pre4 + mm(p34[(1 + a) * 8:(1 + a) * 8 + 40, :].astype(BF), t4[a])
+    pre4 = joint([p34[(1 + a) * 8:(1 + a) * 8 + 40, :].astype(BF) for a in range(3)], weights, "t4")
     act4 = silu_of(pre4)[16:24].astype(BF)
 
-    skip3 = (act3[96:128, :].astype(F32) + enlarged(mm_nt(act4, f4[...]), 8)).astype(BF)
-    skip2 = (act2[512:640, :].astype(F32) + enlarged(mm_nt(skip3, f3[...]), 16)).astype(BF)
-    up2 = mm_nt(skip2, f2[...])
+    skip3 = (act3[96:128, :].astype(F32) + enlarged(mm_nt(act4, taken(weights, "f4")), 8)).astype(BF)
+    skip2 = (act2[512:640, :].astype(F32) + enlarged(mm_nt(skip3, taken(weights, "f3")), 16)).astype(BF)
+    up2 = mm_nt(skip2, taken(weights, "f2"))
     for half in range(2):
         base = act1[2048 + half * 256:2304 + half * 256, :].astype(F32)
         up = enlarged(up2[half * 64:(half + 1) * 64], 32)
@@ -434,7 +414,7 @@
     gh = mm_tn(xc[2048:2560, :], skip1[...])
 
     def fine_carry(step, _):
-        back = mm(xc[rows((16 + step * 8) * 64, 512, 512), :], hp[...]).astype(BF)
+        back = mm(xc[rows((16 + step * 8) * 64, 512, 512), :], taken(weights, "hp")).astype(BF)
         carry2[rows((8 + step * 4) * 32, 128, 128), :] = pooled(back, pool1, 64).astype(BF)
         return 0
 
@@ -442,10 +422,10 @@
 
     for step in range(5):
         start = (8 + step * 4) * 32
-        back = mm(carry2[start:start + 128, :], b2[...]).astype(BF)
+        back = mm(carry2[start:start + 128, :], taken(weights, "b2")).astype(BF)
         back2[start:start + 128, :] = back
         carry3[step * 32:(step + 1) * 32, :] = pooled(back, pool2, 32).astype(BF)
-    back = mm(carry3[...], b3[...]).astype(BF)
+    back = mm(carry3[...], taken(weights, "b3")).astype(BF)
     back3[...] = back
     carry4 = pooled(back, pool3, 16)
 
@@ -453,7 +433,7 @@
     gl3 = mm_tn(carry3[64:96, :], skip3)
     gl4 = mm_tn(carry4[16:24].astype(BF), act4)
 
-    delta4 = (mm(carry4.astype(BF), b4[...]) * slope_of(pre4)).astype(BF).astype(F32)
+    delta4 = (mm(carry4.astype(BF), taken(weights, "b4")) * slope_of(pre4)).astype(BF).astype(F32)
     d4[...] = delta4
     own4 = delta4[16:24].astype(BF)
 
@@ -464,9 +444,7 @@
             + shift_y(total[:, 256:384], count, -1)
         )
 
-    total = mm_nt(d4[16:40, :].astype(BF), t4[0])
-    for a in (1, 2):
-        total = total + mm_nt(d4[(2 - a) * 8:(2 - a) * 8 + 24, :].astype(BF), t4[a])
+    total = joint_nt([d4[(2 - a) * 8:(2 - a) * 8 + 24, :].astype(BF) for a in range(3)], weights, "t4")
     ret4 = returned(total, 8)
 
     def spread_up(field, matrix, count):
@@ -475,28 +453,22 @@
 
     slope = back3[32:128, :].astype(F32) + spread_up(ret4, pool3, 8)
     d3[...] = (slope * slope_of(pre3[64:160, :])).astype(BF)
-    total = mm_nt(d3[32:96, :], t3[0])
-    for a in (1, 2):
-        total = total + mm_nt(d3[(2 - a) * 16:(2 - a) * 16 + 64, :], t3[a])
+    total = joint_nt([d3[(2 - a) * 16:(2 - a) * 16 + 64, :] for a in range(3)], weights, "t3")
     ret3 = returned(total, 16)
 
     slope = back2[14 * 32:22 * 32, :].astype(F32) + spread_up(ret3, pool2, 16)
     d2[...] = (slope * slope_of(pre2[14 * 32:22 * 32, :])).astype(BF)
-    total = mm_nt(d2[64:256, :], t2[0])
-    for a in (1, 2):
-        total = total + mm_nt(d2[(2 - a) * 32:(2 - a) * 32 + 192, :], t2[a])
+    total = joint_nt([d2[(2 - a) * 32:(2 - a) * 32 + 192, :] for a in range(3)], weights, "t2")
     ret2[...] = returned(total, 32)
 
     for step in range(3):
         spot = slice((30 + step * 4) * 64, (34 + step * 4) * 64)
         up = spread_up(ret2[step * 64:(step + 1) * 64, :], pool1, 32)
-        back = mm(xc[spot, :], hp[...]).astype(BF).astype(F32)
+        back = mm(xc[spot, :], taken(weights, "hp")).astype(BF).astype(F32)
         d1[step * 256:(step + 1) * 256, :] = ((back + up) * slope_of(pre1[spot, :])).astype(BF)
 
-    guess = mm_nt(skip1[...], hp[...])
-    total = mm_nt(d1[192:704, :], t1[0])
-    for a in (1, 2):
-        total = total + mm_nt(d1[(3 - a) * 64:(3 - a) * 64 + 512, :], t1[a])
+    guess = mm_nt(skip1[...], taken(weights, "hp"))
+    total = joint_nt([d1[(3 - a) * 64:(3 - a) * 64 + 512, :] for a in range(3)], weights, "t1")
     low, high = total[:, 0:128], total[:, 128:256]
     grad = shift_y(low, 64, 1) + pltpu.roll(low, 80, 1) + shift_y(high, 64, -1)
     line[...] = jnp.where(lane < 48, grad, guess)
@@ -580,11 +552,18 @@
     lift4 = fold_lift(gl4, 64, 128, fold4)
     pack[2224:2288, :] += jnp.where(lane >= 64, pltpu.roll(lift4, 64, 1), 0.0)
     pack[2288:2352, :] += jnp.where(lane >= 64, lift4, 0.0)
-    share_ref[...] = pack[rows(own_part * SHARE, SHARE, SHARE), :].astype(BF)
-
-
-def unpack_kernel(full_ref, order_ref, g1_ref, g2_ref, g3_ref, g4_ref, l4_ref, l3_ref, l2_ref, head_ref):
+    share_ref[...] = pack[rows(where_ref[9] * SHARE, SHARE, SHARE), :].astype(BF)
+
+
+def unpack_kernel(
+    full_ref, g1_ref, g2_ref, g3_ref, g4_ref, l4_ref, l3_ref, l2_ref, head_ref
+):
     scale = float(512 * 64 * 16) ** -0.5
+    row, col = iota((144, 128), 0), iota((144, 128), 1)
+    a_step, spot = row >> 4, row & 15
+    b_row, a_row = (spot * 11) >> 5, (a_step * 11) >> 5
+    tap = 9 * a_row + 3 * b_row + a_step - 3 * a_row
+    chan = jnp.where(spot < 9, spot - 3 * b_row, -1)
 
     def left(start, count):
         return full_ref[start:start + count, :].astype(F32) * scale
@@ -597,7 +576,7 @@
     g3_ref[832:864, :] = right(2352, 32)[:, 0:64]
     g2_ref[...] = right(1728, 432)[:, 0:32]
     for c in range(3):
-        turned = mm_tn(full_ref[1728:1872, :], order_ref[c]) * scale
+        turned = mm_tn(full_ref[1728:1872, :], one_hot((chan == c) & (col == tap))) * scale
         g1_ref[c] = turned[96:112, 0:27]
     l3_ref[...] = right(2160, 32)[:, 0:64]
     l2_ref[...] = right(2192, 16)[:, 0:32]
@@ -606,21 +585,11 @@
     l4_ref[:, 64:128] = left(2288, 64)[:, 64:128]
 
 
-def order_matrix():
-    order = np.zeros((3, 144, 128), np.float32)
-    for tap in range(27):
-        a, b, step = tap // 9, tap // 3 % 3, tap % 3
-        for c in range(3):
-            order[c, (a * 3 + step) * 16 + b * 3 + c, tap] = 1.0
-    return order
-
-
 def run_build(weights, interpret=False):
     k1, k2, k3, k4, l4, l3, l2, head = weights
-    shapes = ((3, 256, 256),) + ((3, 384, 256),) * 3 + ((256, 256),) * 3 + ((128, 256),) * 4
     return pl.pallas_call(
         build_kernel,
-        out_shape=tuple(jax.ShapeDtypeStruct(shape, BF) for shape in shapes),
+        out_shape=jax.ShapeDtypeStruct((WEIGHT_ROWS, 256), BF),
         in_specs=[pl.BlockSpec(memory_space=pltpu.HBM)] * 8,
         scratch_shapes=[
             pltpu.VMEM((128, 256), F32),
@@ -648,7 +617,7 @@
     )
 
 
-def run_main(where, own, tiles, matrices, interpret=False):
+def run_main(where, own, tiles, twins, matrix, interpret=False):
     vm = pl.BlockSpec(memory_space=pltpu.VMEM)
 
     def buf(shape, kind=BF):
@@ -682,20 +651,8 @@
         buf((128, 128), F32),
         buf((512, 128), F32),
         buf((PACK, 128), F32),
-        buf((8, 48, 128)),
-        buf((8, 8, 48, 128)),
-        buf((3, 256, 256)),
-        buf((3, 384, 256)),
-        buf((3, 384, 256)),
-        buf((3, 384, 256)),
-        buf((256, 256)),
-        buf((256, 256)),
-        buf((256, 256)),
-        buf((128, 256)),
-        buf((128, 256)),
-        buf((128, 256)),
-        buf((128, 256)),
-        pltpu.SemaphoreType.DMA((20,)),
+        buf((WEIGHT_ROWS, 256)),
+        pltpu.SemaphoreType.DMA,
     ]
     return pl.pallas_call(
         main_kernel,
@@ -704,17 +661,17 @@
             jax.ShapeDtypeStruct((3, 8, 128), F32),
             jax.ShapeDtypeStruct((SHARE, 128), BF),
         ),
-        in_specs=[pl.BlockSpec(memory_space=pltpu.SMEM)]
-        + [pl.BlockSpec(memory_space=pltpu.HBM)] * 13,
+        in_specs=[pl.BlockSpec(memory_space=pltpu.SMEM)] + [vm] * 3 + [pl.BlockSpec(memory_space=pltpu.HBM)],
         out_specs=(vm, vm, vm),
         scratch_shapes=scratch,
-        compiler_params=pltpu.CompilerParams(vmem_limit_bytes=60 * 1024 * 1024),
+        compiler_params=pltpu.CompilerParams(vmem_limit_bytes=52 * 1024 * 1024),
         interpret=interpret,
     )(
         where,
         own,
         tiles,
-        *matrices,
+        twins,
+        matrix,
     )
 
 
@@ -727,13 +684,12 @@
 
 
 def unpack(full, interpret=False):
-    order = order_matrix()
     shapes = ((3, 16, 27), (432, 32), (864, 64), (1728, 128), (64, 128), (32, 64), (16, 32), (3, 16))
     g1, g2, g3, g4, l4, l3, l2, head = pl.pallas_call(
         unpack_kernel,
         out_shape=tuple(jax.ShapeDtypeStruct(shape, F32) for shape in shapes),
         interpret=interpret,
-    )(full, jnp.asarray(order, BF))
+    )(full)
     return (
         g1.transpose(2, 1, 0),
         g2.reshape(27, 16, 32).transpose(0, 2, 1),
@@ -751,25 +707,35 @@
 GROUP_Z = [[8 * z + y for z in range(8)] for y in range(8)]
 
 
+def shared(x):
+    copies = jnp.broadcast_to(x, (4,) + x.shape)
+    groups = [[0, 2, 4, 6], [1, 3, 5, 7]]
+    return lax.all_to_all(copies, "narrow", 0, 0, axis_index_groups=groups, tiled=True)
+
+
 def exchange(x, groups):
     return lax.all_to_all(x, "wide", 0, 0, axis_index_groups=groups, tiled=True)
 
 
 def local(velocity, cotangent, *weights):
-    where = jnp.stack([lax.axis_index("narrow")] + [4 + step for step in FAR]).astype(jnp.int32)
+    part = lax.axis_index("narrow")
+    even, odd = ([4 + step for step in FAR[core::2]] for core in range(2))
+    order = [jnp.where(part % 2 == 0, a, b) for a, b in zip(even + odd, odd + even)]
+    where = jnp.stack([part] + order + [part // 2]).astype(jnp.int32)
     copies = run_prep(velocity, cotangent)
     own = lax.all_to_all(copies, "narrow", 0, 0, tiled=True)
     routes = [((w + FAR[n]) % 64 * 8 + n, w * 8 + n) for w in range(64) for n in range(8)]
     far = lax.ppermute(own, ("wide", "narrow"), routes)
-    tiles = lax.all_gather(far, "narrow", axis=0)
-    prediction, grad_velocity, share = run_main(where, own, tiles, run_build(weights))
+    far, matrix = lax.optimization_barrier((far, run_build(weights)))
+    tiles = shared(far)
+    twins = lax.ppermute(tiles, "narrow", [(n, n ^ 1) for n in range(8)])
+    prediction, grad_velocity, share = run_main(where, own, tiles, twins, matrix)
     pieces = exchange(share.reshape(8, PIECE, 128), GROUP_Y)
     partial = pieces.astype(F32).sum(axis=0).astype(BF)
     pieces = exchange(jnp.broadcast_to(partial, (8, PIECE, 128)), GROUP_Z)
     total = pieces.astype(F32).sum(axis=0).astype(BF)
     whole = exchange(jnp.broadcast_to(total, (8, PIECE, 128)), GROUP_Y).reshape(SHARE, 128)
-    full = lax.all_gather(whole, "narrow", axis=0).reshape(PACK, 128)
-    return (prediction, grad_velocity) + unpack(full)
+    return (prediction, grad_velocity) + unpack(shared(whole).reshape(PACK, 128))
 
 
 def solution(mesh):

time: 125 us -> 121 us (0.968)
  the two profiles are of different devices: /device:TPU:1 before, /device:TPU:2 now
where the time goes in v3:
time: 121 us; the launch traced here: 120 us
  blocking collectives  77.5 us (64%)
  Pallas kernels  27.8 us (23%)
  waiting for transfers between devices  8.51 us (7%)
  starting transfers between devices  5.29 us (4%)
    all_to_all x3, blocking collectives, exchange(): return lax.all_to_all(x, 'wide', 0, 0, axis_index_groups=groups, tiled=True)  40.8 us
    all_to_all x2, blocking collectives, shared(): lax.all_to_all(copies, 'narrow', 0, 0, axis_index_groups=groups, tiled=True)  23.2 us
    pallas_call x1, Pallas kernels, run_main(): pl.pallas_call(main_kernel, out_shape=(jax.ShapeDtypeStruct((3, 8, 128),...  19.4 us
    all_to_all x1, blocking collectives, local(): own = lax.all_to_all(copies, 'narrow', 0, 0, tiled=True)  13.5 us
    ppermute x1, waiting for transfers between devices, local(): far = lax.ppermute(own, ('wide', 'narrow'), routes)  6.94 us
    pallas_call x1, Pallas kernels, run_build(): pl.pallas_call(build_kernel, out_shape=jax.ShapeDtypeStruct((WEIGHT_ROWS,...  4.1 us
    ppermute x1, starting transfers between devices, local(): far = lax.ppermute(own, ('wide', 'narrow'), routes)  3.38 us
    pallas_call x1, Pallas kernels, unpack(): pl.pallas_call(unpack_kernel, out_shape=tuple((jax.ShapeDtypeStruct(shape...  2.47 us
  transfers between devices with their start and end apart: 2, of which 2 were waited for; matrix products, arithmetic and copies ran while one was open for 0% of the time, Pallas kernels for 3%

profile of v3, /device:TPU:2, one launch (start us, length us, event | category | flops | bytes accessed | tf_op | source)
XLA Modules:
  0.0 120.1 jit_solution(7269639187284775582)
XLA Ops:
  0.6 1.9 %shard_map.177 = bf16[8,48,128]{2,1,0:T(8,128)(2,1)} custom-call(bf16[3,8,128]{2,1,0:T(8,128)(2,1)} %vel_ref.1, bf16[3,8,128]{2,1,0:T(8,128)(2,1)} %cot_ref.1), custom_call_target="tpu_custom_call" | custom-call | tf_op jit(solution)/shard_map/pallas_call | solution.py:679
  2.5 13.5 %all_to_all.30.own_ref = bf16[8,48,128]{2,1,0:T(8,128)(2,1)S(1)} all-to-all(bf16[8,48,128]{2,1,0:T(8,128)(2,1)} %shard_map.177), channel_id=1, replica_groups=mesh['wide'=64,'narrow'=8] {'narrow'}, dimensions={0} | all-to-all | bytes 196608 | tf_op jit(solution)/shard_map/all_to_all | solution.py:726
  16.0 3.4 %collective-permute-start = (bf16[8,48,128]{2,1,0:T(8,128)(2,1)S(1)}, bf16[8,48,128]{2,1,0:T(8,128)(2,1)S(1)}, u32[]{:S(2)}, u32[]{:S(2)}) collective-permute-start(bf16[8,48,128]{2,1,0:T(8,128)(2,1)S(1)} %all_to_all.30.own_ref), channel_id=1, source_target_pairs={{32,0},{505,1},{482,2},{11,3},{28,4},{501,5},{494,6},{23,7},{40,8}... | collective-permute-start | bytes 294920 | tf_op jit(solution)/shard_map/ppermute | solution.py:728
  19.4 4.1 %shard_map.178.weights_far = bf16[5504,256]{1,0:T(8,128)(2,1)} custom-call(bf16[3,16,27]{2,1,0:T(8,128)(2,1)} %bitcast.39, bf16[432,32]{1,0:T(8,128)(2,1)} %bitcast.38, bf16[864,64]{1,0:T(8,128)(2,1)} %bitcast.37, bf16[1728,128]{1,0:T(8,128)(2,1)} %bitcast.36, bf16[64,128]{1,0:T(8,128)(2,1)} %l4_far.1, bf16[32,64]{1,0:T(8,128)(2,1)} %l3_far.1, ...), custom_call_target="tpu_custom_call" | custom-call | tf_op jit(solution)/shard_map/pallas_call | solution.py:590
  23.5 6.9 %collective-permute-done = bf16[8,48,128]{2,1,0:T(8,128)(2,1)S(1)} collective-permute-done((bf16[8,48,128]{2,1,0:T(8,128)(2,1)S(1)}, bf16[8,48,128]{2,1,0:T(8,128)(2,1)S(1)}, u32[]{:S(2)}, u32[]{:S(2)}) %collective-permute-start) | collective-permute-done | bytes 98336 | tf_op jit(solution)/shard_map/ppermute | solution.py:728
  30.5 0.1 broadcast_in_dim.12
  30.5 11.3 %all_to_all.31.tiles_ref = bf16[4,8,48,128]{3,2,1,0:T(8,128)(2,1)S(1)} all-to-all(bf16[4,8,48,128]{3,2,1,0:T(8,128)(2,1)S(1)} %broadcast_in_dim.12), channel_id=1, replica_groups={{0,2,4,6},{1,3,5,7},{8,10,12,14},{9,11,13,15},{16,18,20,22},{17,19,21,2..., dimensions={0} | all-to-all | bytes 786432 | tf_op jit(solution)/shard_map/all_to_all | solution.py:713
  41.8 1.9 %collective-permute-start.1 = (bf16[4,8,48,128]{3,2,1,0:T(8,128)(2,1)S(1)}, bf16[4,8,48,128]{3,2,1,0:T(8,128)(2,1)S(1)}, u32[]{:S(2)}, u32[]{:S(2)}) collective-permute-start(bf16[4,8,48,128]{3,2,1,0:T(8,128)(2,1)S(1)} %all_to_all.31.tiles_ref), channel_id=1, source_target_pairs={{0,1},{1,0},{2,3},{3,2},{4,5},{5,4},{6,7},{7,6},{8,9},{9,8},{10,11... | collective-permute-start | bytes 1179656 | tf_op jit(solution)/shard_map/ppermute | solution.py:731
  43.8 0.1 stack.43.where_ref
  43.9 1.6 %collective-permute-done.1.twins_ref = bf16[4,8,48,128]{3,2,1,0:T(8,128)(2,1)S(1)} collective-permute-done((bf16[4,8,48,128]{3,2,1,0:T(8,128)(2,1)S(1)}, bf16[4,8,48,128]{3,2,1,0:T(8,128)(2,1)S(1)}, u32[]{:S(2)}, u32[]{:S(2)}) %collective-permute-start.1) | collective-permute-done | bytes 393248 | tf_op jit(solution)/shard_map/ppermute | solution.py:731
  45.4 19.4 %shard_map.179 = (f32[3,8,128]{2,1,0:T(8,128)}, f32[3,8,128]{2,1,0:T(8,128)}, bf16[640,128]{1,0:T(8,128)(2,1)S(1)}) custom-call(s32[10]{0:T(128)S(1)} %stack.43.where_ref, bf16[8,48,128]{2,1,0:T(8,128)(2,1)S(1)} %all_to_all.30.own_ref, bf16[4,8,48,128]{3,2,1,0:T(8,128)(2,1)S(1)} %all_to_all.31.tiles_ref, ...), custom_call_target="tpu_custom_call" | custom-call | tf_op jit(solution)/shard_map/pallas_call | solution.py:657
  64.8 12.7 %all_to_all.32 = bf16[8,80,128]{2,1,0:T(8,128)(2,1)S(1)} all-to-all(bf16[8,80,128]{2,1,0:T(8,128)(2,1)S(1)} %bitcast.33), channel_id=1, replica_groups={{0,8,16,24,32,40,48,56},{64,72,80,88,96,104,112,120},{128,136,144,152,1..., dimensions={0} | all-to-all | bytes 327680 | tf_op jit(solution)/shard_map/all_to_all | solution.py:717
  77.6 16.2 %all_to_all.33 = bf16[8,80,128]{2,1,0:T(8,128)(2,1)S(1)} all-to-all(bf16[8,80,128]{2,1,0:T(8,128)(2,1)S(1)} %broadcast_in_dim.13), channel_id=1, replica_groups={{0,64,128,192,256,320,384,448},{8,72,136,200,264,328,392,456},{16,80,14..., dimensions={0} | all-to-all | bytes 327680 | tf_op jit(solution)/shard_map/all_to_all | solution.py:717
  93.9 11.8 %all_to_all.34 = bf16[8,80,128]{2,1,0:T(8,128)(2,1)S(1)} all-to-all(bf16[8,80,128]{2,1,0:T(8,128)(2,1)S(1)} %broadcast_in_dim.14), channel_id=1, replica_groups={{0,8,16,24,32,40,48,56},{64,72,80,88,96,104,112,120},{128,136,144,152,1..., dimensions={0} | all-to-all | bytes 327680 | tf_op jit(solution)/shard_map/all_to_all | solution.py:717
  105.7 0.1 broadcast_in_dim.15
  105.8 11.9 %all_to_all.35 = bf16[4,640,128]{2,1,0:T(8,128)(2,1)} all-to-all(bf16[4,640,128]{2,1,0:T(8,128)(2,1)S(1)} %broadcast_in_dim.15), channel_id=1, replica_groups={{0,2,4,6},{1,3,5,7},{8,10,12,14},{9,11,13,15},{16,18,20,22},{17,19,21,2..., dimensions={0} | all-to-all | bytes 1310720 | tf_op jit(solution)/shard_map/all_to_all | solution.py:713
  117.7 2.5 %shard_map.180 = (f32[3,16,27]{2,1,0:T(8,128)}, f32[432,32]{1,0:T(8,128)}, f32[864,64]{1,0:T(8,128)}, f32[1728,128]{1,0:T(8,128)}, f32[64,128]{1,0:T(8,128)}, /*...) custom-call(bf16[2560,128]{1,0:T(8,128)(2,1)} %bitcast.34), custom_call_target="tpu_custom_call" | custom-call | tf_op jit(solution)/shard_map/pallas_call | solution.py:688
  (4 shorter events, 0.1 us)
Async XLA Ops:
  16.0 14.4 %collective-permute-start = (bf16[8,48,128]{2,1,0:T(8,128)(2,1)S(1)}, bf16[8,48,128]{2,1,0:T(8,128)(2,1)S(1)}, u32[]{:S(2)}, u32[]{:S(2)}) collective-permute-start(bf16[8,48,128]{2,1,0:T(8,128)(2,1)S(1)} %all_to_all.30.own_ref), channel_id=1, source_target_pairs={{32,0},{505,1},{482,2},{11,3},{28,4},{501,5},{494,6},{23,7},{40,8}... | collective-permute-start | bytes 294920 | tf_op jit(solution)/shard_map/ppermute | solution.py:728
  41.8 3.6 %collective-permute-start.1 = (bf16[4,8,48,128]{3,2,1,0:T(8,128)(2,1)S(1)}, bf16[4,8,48,128]{3,2,1,0:T(8,128)(2,1)S(1)}, u32[]{:S(2)}, u32[]{:S(2)}) collective-permute-start(bf16[4,8,48,128]{3,2,1,0:T(8,128)(2,1)S(1)} %all_to_all.31.tiles_ref), channel_id=1, source_target_pairs={{0,1},{1,0},{2,3},{3,2},{4,5},{5,4},{6,7},{7,6},{8,9},{9,8},{10,11... | collective-permute-start | bytes 1179656 | tf_op jit(solution)/shard_map/ppermute | solution.py:731

commit v4 on v3

--- a/solution.py
+++ b/solution.py
@@ -306,7 +306,8 @@
     v3[0:64, :] = jnp.zeros((64, 256), BF)
     v3[73 * 64:74 * 64, :] = jnp.zeros((64, 256), BF)
 
-    def arrange(source, number):
+    def arrange(source, number, slot):
+        lead = slot * 520 + 8
         for n in range(8):
             tile = source(n).astype(F32)
             last = jnp.zeros((16, 128), F32)
@@ -315,39 +316,42 @@
                 last = jnp.where((lane >= 32 * g) & (lane < 32 * g + 32), moved, last)
             for i in range(8):
                 piece = tile[i * 8:i * 8 + 8] if i < 6 else last[(i - 6) * 8:(i - 5) * 8]
-                xt[i * 64 + n * 8:i * 64 + n * 8 + 8, :] = piece
+                xt[lead + i * 64 + n * 8:lead + i * 64 + n * 8 + 8, :] = piece
         for i in range(8):
-            row = xt[i * 64:(i + 1) * 64, :]
+            place = lead + i * 64
+            row = xt[place:place + 64, :]
             xc[rows((number * 8 + i) * 64, 64, 64), :] = row.astype(BF)
-            vel = jnp.where(lane < 48, row, 0.0)
-            low = pltpu.roll(vel, 1, 0) + pltpu.roll(vel, 48, 1)
-            high = pltpu.roll(vel, 63, 0)
+            before = jnp.where(spot_y == 0, row[63:64], xt[place - 1:place + 63, :])
+            after = jnp.where(spot_y == 63, row[0:1], xt[place + 1:place + 65, :])
+            moved = pltpu.roll(row, 48, 1)
+            low = jnp.where(lane < 48, before, jnp.where(lane < 96, moved, 0.0))
+            high = jnp.where(lane < 48, after, 0.0)
             spot = rows((number * 8 + i + 1) * 64, 64, 64)
             v3[spot, 0:128] = low.astype(BF)
             v3[spot, 128:256] = high.astype(BF)
 
-    def arrange_tiles(step, _):
-        arrange(lambda n: tiles_ref[step, n], where_ref[1 + step])
+    def arrange_pairs(turn, _):
+        for half in range(2):
+            step = turn * 2 + half
+            arrange(lambda n: tiles_ref[step, n], where_ref[1 + step], half)
+            arrange(lambda n: twins_ref[step, n], where_ref[5 + step], half + 2)
         return 0
 
-    def arrange_twins(step, _):
-        arrange(lambda n: twins_ref[step, n], where_ref[5 + step])
-        return 0
-
-    arrange(lambda n: own_ref[n], 4)
-    lax.fori_loop(0, 4, arrange_tiles, 0)
-    lax.fori_loop(0, 4, arrange_twins, 0)
+    spot_y = iota((64, 128), 0)
+    arrange(lambda n: own_ref[n], 4, 0)
+    lax.fori_loop(0, 2, arrange_pairs, 0)
     weights_copy.wait()
 
-    def pooled(field, matrix, count):
+    def pooled(field, matrix, count, slot=0):
         flat = mm(field, matrix)
         pairs = field.shape[0] // (2 * count)
+        lead = slot * 256
         for i in range(pairs):
-            tmp[i * count:(i + 1) * count, :] = (
+            tmp[lead + i * count:lead + (i + 1) * count, :] = (
                 flat[2 * i * count:(2 * i + 1) * count] + flat[(2 * i + 1) * count:(2 * i + 2) * count]
             )
         n = pairs * count // 2
-        return tmp[pl.ds(0, n, stride=2), :] + tmp[pl.ds(1, n, stride=2), :]
+        return tmp[pl.ds(lead, n, stride=2), :] + tmp[pl.ds(lead + 1, n, stride=2), :]
 
     def enlarged(field, count):
         n = field.shape[0]
@@ -370,29 +374,33 @@
         ref[spot, 128:256] = field.astype(kind)
         ref[spot, 256:384] = shift_y(field, count, 1).astype(kind)
 
-    def fine_forward(step, _):
-        start = step * 512
-        pre = joint([v3[rows(start + a * 64, 512, 64), :] for a in range(3)], weights, "t1")
-        pre1[rows(start, 512, 512), :] = pre
-        act = silu_of(pre).astype(BF)
-        act1[rows(start, 512, 512), :] = act
-        half = (pooled(act, pool1, 64) * 0.125).astype(BF).astype(F32)
-        put3(p32, step * 128, 32, half, 32)
+    def fine_forward(turn, _):
+        for slot in range(3):
+            step = turn * 3 + slot
+            start = step * 512
+            pre = joint([v3[rows(start + a * 64, 512, 64), :] for a in range(3)], weights, "t1")
+            pre1[rows(start, 512, 512), :] = pre
+            act = silu_of(pre).astype(BF)
+            act1[rows(start, 512, 512), :] = act
+            half = (pooled(act, pool1, 64, slot) * 0.125).astype(BF).astype(F32)
+            put3(p32, step * 128, 32, half, 32)
         return 0
 
-    lax.fori_loop(0, 9, fine_forward, 0)
-
-    def mid_forward(step, _):
-        start = (2 + step * 8) * 32
-        pre = joint([p32[rows(start + (a - 1) * 32, 256, 32), :] for a in range(3)], weights, "t2")
-        pre2[rows(start, 256, 32), :] = pre
-        act = silu_of(pre).astype(BF)
-        act2[rows(start, 256, 32), :] = act
-        half = (pooled(act, pool2, 32) * 0.125).astype(BF).astype(F32)
-        put3(p33, (1 + step * 4) * 16, 16, half, 16)
+    lax.fori_loop(0, 3, fine_forward, 0)
+
+    def mid_forward(turn, _):
+        for slot in range(2):
+            step = turn * 2 + slot
+            start = (2 + step * 8) * 32
+            pre = joint([p32[rows(start + (a - 1) * 32, 256, 32), :] for a in range(3)], weights, "t2")
+            pre2[rows(start, 256, 32), :] = pre
+            act = silu_of(pre).astype(BF)
+            act2[rows(start, 256, 32), :] = act
+            half = (pooled(act, pool2, 32, slot) * 0.125).astype(BF).astype(F32)
+            put3(p33, (1 + step * 4) * 16, 16, half, 16)
         return 0
 
-    lax.fori_loop(0, 4, mid_forward, 0)
+    lax.fori_loop(0, 2, mid_forward, 0)
 
     pre = joint([p33[(1 + a) * 16:(1 + a) * 16 + 224, :] for a in range(3)], weights, "t3")
     pre3[...] = pre
@@ -413,18 +421,15 @@
         skip1[half * 256:(half + 1) * 256, :] = (base + up).astype(BF)
     gh = mm_tn(xc[2048:2560, :], skip1[...])
 
-    def fine_carry(step, _):
-        back = mm(xc[rows((16 + step * 8) * 64, 512, 512), :], taken(weights, "hp")).astype(BF)
-        carry2[rows((8 + step * 4) * 32, 128, 128), :] = pooled(back, pool1, 64).astype(BF)
-        return 0
-
-    lax.fori_loop(0, 5, fine_carry, 0)
+    for step in range(5):
+        back = mm(xc[(16 + step * 8) * 64:(24 + step * 8) * 64, :], taken(weights, "hp")).astype(BF)
+        carry2[(8 + step * 4) * 32:(12 + step * 4) * 32, :] = pooled(back, pool1, 64, step).astype(BF)
 
     for step in range(5):
         start = (8 + step * 4) * 32
         back = mm(carry2[start:start + 128, :], taken(weights, "b2")).astype(BF)
         back2[start:start + 128, :] = back
-        carry3[step * 32:(step + 1) * 32, :] = pooled(back, pool2, 32).astype(BF)
+        carry3[step * 32:(step + 1) * 32, :] = pooled(back, pool2, 32, step).astype(BF)
     back = mm(carry3[...], taken(weights, "b3")).astype(BF)
     back3[...] = back
     carry4 = pooled(back, pool3, 16)
@@ -528,14 +533,27 @@
             part = fold_taps(product, 32, 16, a, b)
             start = 1728 + (a * 3 + b) * 48
             pack[start:start + 48, :] += jnp.where((lane >= 64) & (lane < 96), part, 0.0)
-    fold1 = fold_matrix(256, 16, 96)
+    merged = jnp.zeros((256, 128), F32)
     for a in range(3):
         product = mm_tn(v3[(32 + a) * 64:(40 + a) * 64, :], d1[128:640, :])
         for c in range(3):
-            high, low = halves(jnp.where(band == c, product, 0.0))
-            sums = mm_tn(pick, high) + mm_tn(pick, low)
-            start = 1728 + (a * 3 + c) * 16
-            pack[start:start + 16, :] += mm2(sums, fold1)
+            part = jnp.where(band == c, product, 0.0)
+            part = part[:, 0:128] + part[:, 128:256]
+            for width in (64, 32, 16):
+                part = part + pltpu.roll(part, width, 1)
+            order = a * 3 + c
+            if order < 8:
+                merged = jnp.where((lane >> 4) == order, part, merged)
+    sums = []
+    for field in (merged, part):
+        high, low = halves(field)
+        sums.append(mm_tn(pick, high) + mm_tn(pick, low))
+    for order in range(9):
+        block = sums[order // 8]
+        shift = (96 - order % 8 * 16) % 128
+        block = pltpu.roll(block, shift, 1) if shift else block
+        start = 1728 + order * 16
+        pack[start:start + 16, :] += jnp.where((lane >= 96) & (lane < 112), block, 0.0)
 
     def fold_lift(product, fine, chans, matrix):
         kin = iota((fine, 256), 1) >> log2(chans)
@@ -624,7 +642,7 @@
         return pltpu.VMEM(shape, kind)
 
     scratch = [
-        buf((512, 128), F32),
+        buf((4 * 520 + 16, 128), F32),
         buf((72 * 64, 128)),
         buf((74 * 64, 256)),
         buf((72 * 64, 256), F32),
@@ -646,7 +664,7 @@
         buf((96, 256)),
         buf((40, 256), F32),
         buf((192, 128), F32),
-        buf((256, 128), F32),
+        buf((5 * 256, 128), F32),
         buf((128, 128), F32),
         buf((128, 128), F32),
         buf((512, 128), F32),

time: 121 us -> 119 us (0.983)
  Pallas kernels: 27.8 us -> 25.9 us
    pallas_call x1, Pallas kernels: 19.4 us -> 17.5 us  [run_main(): pl.pallas_call(main_kernel, out_shape=(jax.ShapeDtypeStruct((3, 8, 128),...]
where the time goes in v4:
time: 119 us; the launch traced here: 118 us
  blocking collectives  77.5 us (65%)
  Pallas kernels  25.9 us (22%)
  waiting for transfers between devices  8.51 us (7%)
  starting transfers between devices  5.29 us (4%)
    all_to_all x3, blocking collectives, exchange(): return lax.all_to_all(x, 'wide', 0, 0, axis_index_groups=groups, tiled=True)  40.8 us
    all_to_all x2, blocking collectives, shared(): lax.all_to_all(copies, 'narrow', 0, 0, axis_index_groups=groups, tiled=True)  23.2 us
    pallas_call x1, Pallas kernels, run_main(): pl.pallas_call(main_kernel, out_shape=(jax.ShapeDtypeStruct((3, 8, 128),...  17.5 us
    all_to_all x1, blocking collectives, local(): own = lax.all_to_all(copies, 'narrow', 0, 0, tiled=True)  13.5 us
    ppermute x1, waiting for transfers between devices, local(): far = lax.ppermute(own, ('wide', 'narrow'), routes)  6.94 us
    pallas_call x1, Pallas kernels, run_build(): pl.pallas_call(build_kernel, out_shape=jax.ShapeDtypeStruct((WEIGHT_ROWS,...  4.1 us
    ppermute x1, starting transfers between devices, local(): far = lax.ppermute(own, ('wide', 'narrow'), routes)  3.38 us
    pallas_call x1, Pallas kernels, unpack(): pl.pallas_call(unpack_kernel, out_shape=tuple((jax.ShapeDtypeStruct(shape...  2.47 us
  transfers between devices with their start and end apart: 2, of which 2 were waited for; matrix products, arithmetic and copies ran while one was open for 0% of the time, Pallas kernels for 3%

profile of v4, /device:TPU:2, one launch (start us, length us, event | category | flops | bytes accessed | tf_op | source)
XLA Modules:
  0.0 118.2 jit_solution(1077728891328244229)
XLA Ops:
  0.6 1.9 %shard_map.177 = bf16[8,48,128]{2,1,0:T(8,128)(2,1)} custom-call(bf16[3,8,128]{2,1,0:T(8,128)(2,1)} %vel_ref.1, bf16[3,8,128]{2,1,0:T(8,128)(2,1)} %cot_ref.1), custom_call_target="tpu_custom_call" | custom-call | tf_op jit(solution)/shard_map/pallas_call | solution.py:697
  2.5 13.5 %all_to_all.30.own_ref = bf16[8,48,128]{2,1,0:T(8,128)(2,1)S(1)} all-to-all(bf16[8,48,128]{2,1,0:T(8,128)(2,1)} %shard_map.177), channel_id=1, replica_groups=mesh['wide'=64,'narrow'=8] {'narrow'}, dimensions={0} | all-to-all | bytes 196608 | tf_op jit(solution)/shard_map/all_to_all | solution.py:744
  16.0 3.4 %collective-permute-start = (bf16[8,48,128]{2,1,0:T(8,128)(2,1)S(1)}, bf16[8,48,128]{2,1,0:T(8,128)(2,1)S(1)}, u32[]{:S(2)}, u32[]{:S(2)}) collective-permute-start(bf16[8,48,128]{2,1,0:T(8,128)(2,1)S(1)} %all_to_all.30.own_ref), channel_id=1, source_target_pairs={{32,0},{505,1},{482,2},{11,3},{28,4},{501,5},{494,6},{23,7},{40,8}... | collective-permute-start | bytes 294920 | tf_op jit(solution)/shard_map/ppermute | solution.py:746
  19.4 4.1 %shard_map.178.weights_far = bf16[5504,256]{1,0:T(8,128)(2,1)} custom-call(bf16[3,16,27]{2,1,0:T(8,128)(2,1)} %bitcast.39, bf16[432,32]{1,0:T(8,128)(2,1)} %bitcast.38, bf16[864,64]{1,0:T(8,128)(2,1)} %bitcast.37, bf16[1728,128]{1,0:T(8,128)(2,1)} %bitcast.36, bf16[64,128]{1,0:T(8,128)(2,1)} %l4_far.1, bf16[32,64]{1,0:T(8,128)(2,1)} %l3_far.1, ...), custom_call_target="tpu_custom_call" | custom-call | tf_op jit(solution)/shard_map/pallas_call | solution.py:608
  23.5 6.9 %collective-permute-done = bf16[8,48,128]{2,1,0:T(8,128)(2,1)S(1)} collective-permute-done((bf16[8,48,128]{2,1,0:T(8,128)(2,1)S(1)}, bf16[8,48,128]{2,1,0:T(8,128)(2,1)S(1)}, u32[]{:S(2)}, u32[]{:S(2)}) %collective-permute-start) | collective-permute-done | bytes 98336 | tf_op jit(solution)/shard_map/ppermute | solution.py:746
  30.5 0.1 broadcast_in_dim.12
  30.5 11.3 %all_to_all.31.tiles_ref = bf16[4,8,48,128]{3,2,1,0:T(8,128)(2,1)S(1)} all-to-all(bf16[4,8,48,128]{3,2,1,0:T(8,128)(2,1)S(1)} %broadcast_in_dim.12), channel_id=1, replica_groups={{0,2,4,6},{1,3,5,7},{8,10,12,14},{9,11,13,15},{16,18,20,22},{17,19,21,2..., dimensions={0} | all-to-all | bytes 786432 | tf_op jit(solution)/shard_map/all_to_all | solution.py:731
  41.8 1.9 %collective-permute-start.1 = (bf16[4,8,48,128]{3,2,1,0:T(8,128)(2,1)S(1)}, bf16[4,8,48,128]{3,2,1,0:T(8,128)(2,1)S(1)}, u32[]{:S(2)}, u32[]{:S(2)}) collective-permute-start(bf16[4,8,48,128]{3,2,1,0:T(8,128)(2,1)S(1)} %all_to_all.31.tiles_ref), channel_id=1, source_target_pairs={{0,1},{1,0},{2,3},{3,2},{4,5},{5,4},{6,7},{7,6},{8,9},{9,8},{10,11... | collective-permute-start | bytes 1179656 | tf_op jit(solution)/shard_map/ppermute | solution.py:749
  43.8 0.1 stack.43.where_ref
  43.9 1.6 %collective-permute-done.1.twins_ref = bf16[4,8,48,128]{3,2,1,0:T(8,128)(2,1)S(1)} collective-permute-done((bf16[4,8,48,128]{3,2,1,0:T(8,128)(2,1)S(1)}, bf16[4,8,48,128]{3,2,1,0:T(8,128)(2,1)S(1)}, u32[]{:S(2)}, u32[]{:S(2)}) %collective-permute-start.1) | collective-permute-done | bytes 393248 | tf_op jit(solution)/shard_map/ppermute | solution.py:749
  45.4 17.5 %shard_map.179 = (f32[3,8,128]{2,1,0:T(8,128)}, f32[3,8,128]{2,1,0:T(8,128)}, bf16[640,128]{1,0:T(8,128)(2,1)S(1)}) custom-call(s32[10]{0:T(128)S(1)} %stack.43.where_ref, bf16[8,48,128]{2,1,0:T(8,128)(2,1)S(1)} %all_to_all.30.own_ref, bf16[4,8,48,128]{3,2,1,0:T(8,128)(2,1)S(1)} %all_to_all.31.tiles_ref, ...), custom_call_target="tpu_custom_call" | custom-call | tf_op jit(solution)/shard_map/pallas_call | solution.py:675
  62.9 12.7 %all_to_all.32 = bf16[8,80,128]{2,1,0:T(8,128)(2,1)S(1)} all-to-all(bf16[8,80,128]{2,1,0:T(8,128)(2,1)S(1)} %bitcast.33), channel_id=1, replica_groups={{0,8,16,24,32,40,48,56},{64,72,80,88,96,104,112,120},{128,136,144,152,1..., dimensions={0} | all-to-all | bytes 327680 | tf_op jit(solution)/shard_map/all_to_all | solution.py:735
  75.7 16.2 %all_to_all.33 = bf16[8,80,128]{2,1,0:T(8,128)(2,1)S(1)} all-to-all(bf16[8,80,128]{2,1,0:T(8,128)(2,1)S(1)} %broadcast_in_dim.13), channel_id=1, replica_groups={{0,64,128,192,256,320,384,448},{8,72,136,200,264,328,392,456},{16,80,14..., dimensions={0} | all-to-all | bytes 327680 | tf_op jit(solution)/shard_map/all_to_all | solution.py:735
  92.0 11.8 %all_to_all.34 = bf16[8,80,128]{2,1,0:T(8,128)(2,1)S(1)} all-to-all(bf16[8,80,128]{2,1,0:T(8,128)(2,1)S(1)} %broadcast_in_dim.14), channel_id=1, replica_groups={{0,8,16,24,32,40,48,56},{64,72,80,88,96,104,112,120},{128,136,144,152,1..., dimensions={0} | all-to-all | bytes 327680 | tf_op jit(solution)/shard_map/all_to_all | solution.py:735
  103.8 0.1 broadcast_in_dim.15
  103.9 11.9 %all_to_all.35 = bf16[4,640,128]{2,1,0:T(8,128)(2,1)} all-to-all(bf16[4,640,128]{2,1,0:T(8,128)(2,1)S(1)} %broadcast_in_dim.15), channel_id=1, replica_groups={{0,2,4,6},{1,3,5,7},{8,10,12,14},{9,11,13,15},{16,18,20,22},{17,19,21,2..., dimensions={0} | all-to-all | bytes 1310720 | tf_op jit(solution)/shard_map/all_to_all | solution.py:731
  115.8 2.5 %shard_map.180 = (f32[3,16,27]{2,1,0:T(8,128)}, f32[432,32]{1,0:T(8,128)}, f32[864,64]{1,0:T(8,128)}, f32[1728,128]{1,0:T(8,128)}, f32[64,128]{1,0:T(8,128)}, /*...) custom-call(bf16[2560,128]{1,0:T(8,128)(2,1)} %bitcast.34), custom_call_target="tpu_custom_call" | custom-call | tf_op jit(solution)/shard_map/pallas_call | solution.py:706
  (4 shorter events, 0.1 us)
Async XLA Ops:
  16.0 14.4 %collective-permute-start = (bf16[8,48,128]{2,1,0:T(8,128)(2,1)S(1)}, bf16[8,48,128]{2,1,0:T(8,128)(2,1)S(1)}, u32[]{:S(2)}, u32[]{:S(2)}) collective-permute-start(bf16[8,48,128]{2,1,0:T(8,128)(2,1)S(1)} %all_to_all.30.own_ref), channel_id=1, source_target_pairs={{32,0},{505,1},{482,2},{11,3},{28,4},{501,5},{494,6},{23,7},{40,8}... | collective-permute-start | bytes 294920 | tf_op jit(solution)/shard_map/ppermute | solution.py:746
  41.8 3.6 %collective-permute-start.1 = (bf16[4,8,48,128]{3,2,1,0:T(8,128)(2,1)S(1)}, bf16[4,8,48,128]{3,2,1,0:T(8,128)(2,1)S(1)}, u32[]{:S(2)}, u32[]{:S(2)}) collective-permute-start(bf16[4,8,48,128]{3,2,1,0:T(8,128)(2,1)S(1)} %all_to_all.31.tiles_ref), channel_id=1, source_target_pairs={{0,1},{1,0},{2,3},{3,2},{4,5},{5,4},{6,7},{7,6},{8,9},{9,8},{10,11... | collective-permute-start | bytes 1179656 | tf_op jit(solution)/shard_map/ppermute | solution.py:749

commit v5 on v4

--- a/solution.py
+++ b/solution.py
@@ -720,7 +720,7 @@
     )
 
 
-FAR = (4, -1, -4, 1, 3, -2, -3, 2)
+FAR = (-1, 4, 1, -4, -2, 3, 2, -3)
 GROUP_Y = [[8 * z + y for y in range(8)] for z in range(8)]
 GROUP_Z = [[8 * z + y for z in range(8)] for y in range(8)]
 

time: 119 us -> 117 us (0.983)
  waiting for transfers between devices: 8.51 us -> 1.46 us
  starting transfers between devices: 5.29 us -> 11.5 us
    ppermute x1, waiting for transfers between devices: 6.94 us -> 0.01 us  [local(): far = lax.ppermute(own, ('wide', 'narrow'), routes)]
    ppermute x1, starting transfers between devices: 3.38 us -> 9.5 us  [local(): far = lax.ppermute(own, ('wide', 'narrow'), routes)]
    all_to_all x3, blocking collectives: 40.8 us -> 39.2 us  [exchange(): return lax.all_to_all(x, 'wide', 0, 0, axis_index_groups=groups, tiled=True)]
  transfers between devices with their start and end apart: 2 -> 2, of which waited for: 2 -> 1; matrix products, arithmetic and copies ran while one was open for 0% -> 0% of each run, Pallas kernels for 3% -> 4%
where the time goes in v5:
time: 117 us
  blocking collectives  77 us (66%)
  Pallas kernels  25.9 us (22%)
  starting transfers between devices  11.5 us (10%)
  waiting for transfers between devices  1.46 us (1%)
    all_to_all x3, blocking collectives, exchange(): return lax.all_to_all(x, 'wide', 0, 0, axis_index_groups=groups, tiled=True)  39.2 us
    all_to_all x2, blocking collectives, shared(): lax.all_to_all(copies, 'narrow', 0, 0, axis_index_groups=groups, tiled=True)  24.2 us
    pallas_call x1, Pallas kernels, run_main(): pl.pallas_call(main_kernel, out_shape=(jax.ShapeDtypeStruct((3, 8, 128),...  17.5 us
    all_to_all x1, blocking collectives, local(): own = lax.all_to_all(copies, 'narrow', 0, 0, tiled=True)  13.5 us
    ppermute x1, starting transfers between devices, local(): far = lax.ppermute(own, ('wide', 'narrow'), routes)  9.5 us
    pallas_call x1, Pallas kernels, run_build(): pl.pallas_call(build_kernel, out_shape=jax.ShapeDtypeStruct((WEIGHT_ROWS,...  4.1 us
    pallas_call x1, Pallas kernels, unpack(): pl.pallas_call(unpack_kernel, out_shape=tuple((jax.ShapeDtypeStruct(shape...  2.47 us
  transfers between devices with their start and end apart: 2, of which 1 were waited for; matrix products, arithmetic and copies ran while one was open for 0% of the time, Pallas kernels for 4%

profile of v5, /device:TPU:2, one launch (start us, length us, event | category | flops | bytes accessed | tf_op | source)
XLA Modules:
  0.0 116.9 jit_solution(10929999288289108404)
XLA Ops:
  0.6 1.9 %shard_map.177 = bf16[8,48,128]{2,1,0:T(8,128)(2,1)} custom-call(bf16[3,8,128]{2,1,0:T(8,128)(2,1)} %vel_ref.1, bf16[3,8,128]{2,1,0:T(8,128)(2,1)} %cot_ref.1), custom_call_target="tpu_custom_call" | custom-call | tf_op jit(solution)/shard_map/pallas_call | solution.py:697
  2.5 13.5 %all_to_all.30.own_ref = bf16[8,48,128]{2,1,0:T(8,128)(2,1)S(1)} all-to-all(bf16[8,48,128]{2,1,0:T(8,128)(2,1)} %shard_map.177), channel_id=1, replica_groups=mesh['wide'=64,'narrow'=8] {'narrow'}, dimensions={0} | all-to-all | bytes 196608 | tf_op jit(solution)/shard_map/all_to_all | solution.py:744
  16.0 9.5 %collective-permute-start = (bf16[8,48,128]{2,1,0:T(8,128)(2,1)S(1)}, bf16[8,48,128]{2,1,0:T(8,128)(2,1)S(1)}, u32[]{:S(2)}, u32[]{:S(2)}) collective-permute-start(bf16[8,48,128]{2,1,0:T(8,128)(2,1)S(1)} %all_to_all.30.own_ref), channel_id=1, source_target_pairs={{504,0},{33,1},{10,2},{483,3},{500,4},{29,5},{22,6},{495,7},{0,8},... | collective-permute-start | bytes 294920 | tf_op jit(solution)/shard_map/ppermute | solution.py:746
  25.5 4.1 %shard_map.178.weights_far = bf16[5504,256]{1,0:T(8,128)(2,1)} custom-call(bf16[3,16,27]{2,1,0:T(8,128)(2,1)} %bitcast.39, bf16[432,32]{1,0:T(8,128)(2,1)} %bitcast.38, bf16[864,64]{1,0:T(8,128)(2,1)} %bitcast.37, bf16[1728,128]{1,0:T(8,128)(2,1)} %bitcast.36, bf16[64,128]{1,0:T(8,128)(2,1)} %l4_far.1, bf16[32,64]{1,0:T(8,128)(2,1)} %l3_far.1, ...), custom_call_target="tpu_custom_call" | custom-call | tf_op jit(solution)/shard_map/pallas_call | solution.py:608
  29.6 0.0 collective-permute-done
  29.6 0.1 broadcast_in_dim.12
  29.7 12.3 %all_to_all.31.tiles_ref = bf16[4,8,48,128]{3,2,1,0:T(8,128)(2,1)S(1)} all-to-all(bf16[4,8,48,128]{3,2,1,0:T(8,128)(2,1)S(1)} %broadcast_in_dim.12), channel_id=1, replica_groups={{0,2,4,6},{1,3,5,7},{8,10,12,14},{9,11,13,15},{16,18,20,22},{17,19,21,2..., dimensions={0} | all-to-all | bytes 786432 | tf_op jit(solution)/shard_map/all_to_all | solution.py:731
  42.0 2.0 %collective-permute-start.1 = (bf16[4,8,48,128]{3,2,1,0:T(8,128)(2,1)S(1)}, bf16[4,8,48,128]{3,2,1,0:T(8,128)(2,1)S(1)}, u32[]{:S(2)}, u32[]{:S(2)}) collective-permute-start(bf16[4,8,48,128]{3,2,1,0:T(8,128)(2,1)S(1)} %all_to_all.31.tiles_ref), channel_id=1, source_target_pairs={{0,1},{1,0},{2,3},{3,2},{4,5},{5,4},{6,7},{7,6},{8,9},{9,8},{10,11... | collective-permute-start | bytes 1179656 | tf_op jit(solution)/shard_map/ppermute | solution.py:749
  44.1 0.1 stack.43.where_ref
  44.2 1.5 %collective-permute-done.1.twins_ref = bf16[4,8,48,128]{3,2,1,0:T(8,128)(2,1)S(1)} collective-permute-done((bf16[4,8,48,128]{3,2,1,0:T(8,128)(2,1)S(1)}, bf16[4,8,48,128]{3,2,1,0:T(8,128)(2,1)S(1)}, u32[]{:S(2)}, u32[]{:S(2)}) %collective-permute-start.1) | collective-permute-done | bytes 393248 | tf_op jit(solution)/shard_map/ppermute | solution.py:749
  45.6 17.5 %shard_map.179 = (f32[3,8,128]{2,1,0:T(8,128)}, f32[3,8,128]{2,1,0:T(8,128)}, bf16[640,128]{1,0:T(8,128)(2,1)S(1)}) custom-call(s32[10]{0:T(128)S(1)} %stack.43.where_ref, bf16[8,48,128]{2,1,0:T(8,128)(2,1)S(1)} %all_to_all.30.own_ref, bf16[4,8,48,128]{3,2,1,0:T(8,128)(2,1)S(1)} %all_to_all.31.tiles_ref, ...), custom_call_target="tpu_custom_call" | custom-call | tf_op jit(solution)/shard_map/pallas_call | solution.py:675
  63.1 12.7 %all_to_all.32 = bf16[8,80,128]{2,1,0:T(8,128)(2,1)S(1)} all-to-all(bf16[8,80,128]{2,1,0:T(8,128)(2,1)S(1)} %bitcast.33), channel_id=1, replica_groups={{0,8,16,24,32,40,48,56},{64,72,80,88,96,104,112,120},{128,136,144,152,1..., dimensions={0} | all-to-all | bytes 327680 | tf_op jit(solution)/shard_map/all_to_all | solution.py:735
  75.9 14.7 %all_to_all.33 = bf16[8,80,128]{2,1,0:T(8,128)(2,1)S(1)} all-to-all(bf16[8,80,128]{2,1,0:T(8,128)(2,1)S(1)} %broadcast_in_dim.13), channel_id=1, replica_groups={{0,64,128,192,256,320,384,448},{8,72,136,200,264,328,392,456},{16,80,14..., dimensions={0} | all-to-all | bytes 327680 | tf_op jit(solution)/shard_map/all_to_all | solution.py:735
  90.6 11.8 %all_to_all.34 = bf16[8,80,128]{2,1,0:T(8,128)(2,1)S(1)} all-to-all(bf16[8,80,128]{2,1,0:T(8,128)(2,1)S(1)} %broadcast_in_dim.14), channel_id=1, replica_groups={{0,8,16,24,32,40,48,56},{64,72,80,88,96,104,112,120},{128,136,144,152,1..., dimensions={0} | all-to-all | bytes 327680 | tf_op jit(solution)/shard_map/all_to_all | solution.py:735
  102.5 0.1 broadcast_in_dim.15
  102.6 11.9 %all_to_all.35 = bf16[4,640,128]{2,1,0:T(8,128)(2,1)} all-to-all(bf16[4,640,128]{2,1,0:T(8,128)(2,1)S(1)} %broadcast_in_dim.15), channel_id=1, replica_groups={{0,2,4,6},{1,3,5,7},{8,10,12,14},{9,11,13,15},{16,18,20,22},{17,19,21,2..., dimensions={0} | all-to-all | bytes 1310720 | tf_op jit(solution)/shard_map/all_to_all | solution.py:731
  114.4 2.5 %shard_map.180 = (f32[3,16,27]{2,1,0:T(8,128)}, f32[432,32]{1,0:T(8,128)}, f32[864,64]{1,0:T(8,128)}, f32[1728,128]{1,0:T(8,128)}, f32[64,128]{1,0:T(8,128)}, /*...) custom-call(bf16[2560,128]{1,0:T(8,128)(2,1)} %bitcast.34), custom_call_target="tpu_custom_call" | custom-call | tf_op jit(solution)/shard_map/pallas_call | solution.py:706
  (4 shorter events, 0.1 us)
Async XLA Ops:
  16.0 13.6 %collective-permute-start = (bf16[8,48,128]{2,1,0:T(8,128)(2,1)S(1)}, bf16[8,48,128]{2,1,0:T(8,128)(2,1)S(1)}, u32[]{:S(2)}, u32[]{:S(2)}) collective-permute-start(bf16[8,48,128]{2,1,0:T(8,128)(2,1)S(1)} %all_to_all.30.own_ref), channel_id=1, source_target_pairs={{504,0},{33,1},{10,2},{483,3},{500,4},{29,5},{22,6},{495,7},{0,8},... | collective-permute-start | bytes 294920 | tf_op jit(solution)/shard_map/ppermute | solution.py:746
  42.0 3.6 %collective-permute-start.1 = (bf16[4,8,48,128]{3,2,1,0:T(8,128)(2,1)S(1)}, bf16[4,8,48,128]{3,2,1,0:T(8,128)(2,1)S(1)}, u32[]{:S(2)}, u32[]{:S(2)}) collective-permute-start(bf16[4,8,48,128]{3,2,1,0:T(8,128)(2,1)S(1)} %all_to_all.31.tiles_ref), channel_id=1, source_target_pairs={{0,1},{1,0},{2,3},{3,2},{4,5},{5,4},{6,7},{7,6},{8,9},{9,8},{10,11... | collective-permute-start | bytes 1179656 | tf_op jit(solution)/shard_map/ppermute | solution.py:749
